TPU v7x, 32 devices: a whole 2x2x4 slice. The times are simulated.
32 devices in a mesh: aa: 8 (over z, x), ba: 4 (over y, core).
Axes of the slice: x: 2, y: 2, z: 4, core: 2. Of those that a mesh axis runs over, the one named last changes fastest.
Arguments:
- grid_fields: bfloat16 [1920, 36, 3072], P('aa', None, 'ba'), may hold values from -6 to 6
- band_rows: int32 [8], replicated, may hold values from 1 to 240, 1280 in all
- wave_owner: int32 [640], replicated, may hold values from 0 to 639, each once
- lower_blocks: float32 [3, 3, 12], replicated, may hold values from -0.3 to 0.3
- pivot_inverse: float32 [3, 3, 12], replicated, may hold values from -0.2 to 1.1, as said below
- upper_blocks: float32 [3, 3, 12], replicated, may hold values from -0.3 to 0.3
- legendre: bfloat16 [640, 1280, 896], P(('aa', 'ba')), may hold values from -0.0029296875 to 0.0029296875
Outputs:
- spectral: float32 [640, 72, 896], P(('aa', 'ba'))
Inputs may be any that keep to these rules, and one draw needn't show every extreme that they name: The latitudes of band d fill its first band_rows[d] row slots in order; the bands' counts add up to 1280; row slots past a band's count are never read. `wave_owner`: each wavenumber 0 to 639 appears once. `pivot_inverse`: diagonal entries lie in 0.6 to 1.1, the others within -0.2 to 0.2.
All inputs are finite; a program needn't handle non-finite values.
Results may differ from a plain program's by a relative error of at most 0.0047.
Values may be sent and summed in bfloat16 or wider, within the bound.
A program may use at most 192 MiB of HBM per device.

v0:
```python
import math

import jax
import jax.numpy as jnp
from jax import lax
from jax.sharding import PartitionSpec as P

NLON = 3072
NLAT = 1280
M = 640
NDEG = 896
NT = 1279


def apply_block(block, vector):
    width = vector.shape[1]
    outputs = []
    for row_index in range(width):
        total = block[row_index, 0] * vector[:, 0]
        for col_index in range(1, width):
            total = total + block[row_index, col_index] * vector[:, col_index]
        outputs.append(total)
    return jnp.stack(outputs, axis=1)


def block_product(left_blocks, right_blocks):
    width = left_blocks.shape[0]
    rows_out = []
    for row_index in range(width):
        cols_out = []
        for col_index in range(width):
            total = left_blocks[row_index, 0] * right_blocks[0, col_index]
            for inner in range(1, width):
                total = total + left_blocks[row_index, inner] * right_blocks[inner, col_index]
            cols_out.append(total)
        rows_out.append(jnp.stack(cols_out, axis=0))
    return jnp.stack(rows_out, axis=0)


def diffuse(band, lower_blocks, pivot_inverse, upper_blocks):
    slot_rows, lf_total, lon_width = band.shape
    levels = lower_blocks.shape[2]
    fields = lf_total // levels
    values = band.astype(jnp.float32).reshape(slot_rows, fields, levels, lon_width)
    values = jnp.moveaxis(values, 2, 0)
    coupling = block_product(pivot_inverse, upper_blocks)
    lower_seq = jnp.moveaxis(lower_blocks, 2, 0)
    inverse_seq = jnp.moveaxis(pivot_inverse, 2, 0)
    coupling_seq = jnp.moveaxis(coupling, 2, 0)

    def forward(carry, inputs):
        source, lower_lev, inverse_lev = inputs
        sweep = apply_block(inverse_lev, source - apply_block(lower_lev, carry))
        return (sweep, sweep)

    zero_state = jnp.zeros(values.shape[1:], jnp.float32)
    last_sweep, sweeps = lax.scan(forward, zero_state, (values, lower_seq, inverse_seq))

    def backward(carry, inputs):
        sweep, coupling_lev = inputs
        result = sweep - apply_block(coupling_lev, carry)
        return (result, result)

    last_solved, solved = lax.scan(backward, zero_state, (sweeps, coupling_seq), reverse=True)
    solved = jnp.moveaxis(solved, 0, 2).reshape(slot_rows, lf_total, lon_width)
    return solved.astype(jnp.bfloat16)


def fourier_table(wave_owner, lon_total):
    lon_index = jnp.arange(lon_total, dtype=jnp.int32)
    phase = wave_owner[:, None] * lon_index[None, :] % lon_total
    angle = phase.astype(jnp.float32) * (2.0 * math.pi / lon_total)
    return jnp.stack([jnp.cos(angle), -jnp.sin(angle)]).astype(jnp.bfloat16)


def latitude_slots(band_rows, slot_rows, lat_total):
    band_ends = jnp.cumsum(band_rows)
    starts = band_ends - band_rows
    latitude = jnp.arange(lat_total, dtype=jnp.int32)
    band_index = jnp.sum((band_ends[None, :] <= latitude[:, None]).astype(jnp.int32), axis=1)
    in_band = band_index[:, None] == jnp.arange(band_rows.shape[0], dtype=jnp.int32)[None, :]
    band_start = jnp.sum(jnp.where(in_band, starts[None, :], 0), axis=1)
    return band_index * slot_rows + latitude - band_start


def shards(grid_fields, band_rows, wave_owner, lower_blocks, pivot_inverse, upper_blocks, legendre):
    smooth = diffuse(grid_fields, lower_blocks, pivot_inverse, upper_blocks)
    dft_table = fourier_table(wave_owner, NLON)
    slot_rows = smooth.shape[0]
    group_count = lax.axis_size("ba")
    band_count = lax.axis_size("aa")
    quarter = smooth.shape[1] // group_count
    circles = lax.all_to_all(smooth, "ba", split_axis=1, concat_axis=2, tiled=True)
    flat_rows = circles.reshape(slot_rows * quarter, NLON)
    fourier = jnp.dot(
        dft_table.reshape(2 * M, NLON), flat_rows.T, preferred_element_type=jnp.float32
    )
    fourier = fourier.astype(jnp.bfloat16).reshape(2, M, slot_rows, quarter)
    per_device = M // (band_count * group_count)
    arrived = lax.all_to_all(fourier[None], ("aa", "ba"), split_axis=2, concat_axis=0, tiled=True)
    arrived = arrived.reshape(band_count, group_count, 2, per_device, slot_rows, quarter)
    panels = jnp.transpose(arrived, (3, 2, 1, 5, 0, 4)).reshape(
        per_device, 2 * group_count * quarter, band_count * slot_rows
    )
    lat_slot = latitude_slots(band_rows, slot_rows, NLAT)
    panels = jnp.take(panels, lat_slot, axis=2)
    spectral = jnp.einsum("scl,sln->scn", panels, legendre, preferred_element_type=jnp.float32)
    first_slot = (lax.axis_index("aa") * group_count + lax.axis_index("ba")) * per_device
    owners = lax.dynamic_slice_in_dim(wave_owner, first_slot, per_device)
    kept_mask = jnp.arange(NDEG, dtype=jnp.int32)[None, :] + owners[:, None] <= NT
    return jnp.where(kept_mask[:, None, :], spectral, 0.0)


def solution(mesh):
    placed = (P("aa", None, "ba"), P(), P(), P(), P(), P(), P(("aa", "ba"), None, None))
    return jax.shard_map(
        shards, mesh=mesh, in_specs=placed, out_specs=P(("aa", "ba"), None, None), check_vma=False
    )
```

profile of v0, /device:TPU:0, one launch (start us, length us, event | category | flops | bytes accessed | tf_op | source)
XLA Modules:
  0.0 1144.3 jit_solution(12246874670395878043)
XLA Ops:
  3.6 14.7 %convert_bitcast_fusion = f32[12,240,3,768]{3,1,0,2:T(8,128)} fusion(bf16[240,3,12,768]{3,0,2,1:T(8,128)(2,1)} %bitcast.183), kind=kLoop, calls=%fused_computation.22 | loop fusion | flops 6635520 | bytes 39813120 | tf_op jit(solution)/shard_map/transpose | solution.py:45
  20.3 423.8 %while.29 = (s32[]{:T(128)}, f32[240,3,768]{2,1,0:T(4,128)}, f32[12,240,3,768]{3,2,1,0:T(4,128)}, f32[12,3,3]{2,1,0:T(4,128)S(1)}, f32[12,240,3,768]{3,1,0,2:T(8,128)}, /*index=5*/f32[12,3,3]{2,1,0:T(4,128)S(1)}, s32[]{:T(128)}) while((s32[]{:T(128)}, f32[240,3,768]{2,1,0:T(4,128)}, f32[12,240,3,768]{3,2,1,0:T(4,128)}, ...), condition=%wide.region_4.5_spmd, body=%wide.region_3.4_spmd.sunk | while | flops 8294402 | bytes 28017596 | solution.py:57
  21.0 13.1 %multiply_add_fusion.12 = (f32[240,1,768]{2,1,0:T(1,128)S(1)}, f32[240,1,768]{2,1,0:T(1,128)S(1)}, f32[240,1,768]{2,1,0:T(1,128)S(1)}) fusion(f32[]{:T(128)} %bitcast.147, f32[]{:T(128)} %bitcast.148, f32[]{:T(128)} %bitcast.149, f32[240,3,768]{2,1,0:T(4,128)} %get-tuple-element.429, f32[]{:T(128)} %bitcast.150, f32[]{:T(128)} %bitcast.151, ...), kind=kLoop, calls=%fused_computation.10.clone.1 | loop fusion | flops 2764800 | bytes 4423716 | tf_op jit(solution)/shard_map/while/body/eval_jaxpr/add | solution.py:21
  56.3 13.1 %multiply_add_fusion.12 = (f32[240,1,768]{2,1,0:T(1,128)S(1)}, f32[240,1,768]{2,1,0:T(1,128)S(1)}, f32[240,1,768]{2,1,0:T(1,128)S(1)}) fusion(f32[]{:T(128)} %bitcast.147, f32[]{:T(128)} %bitcast.148, f32[]{:T(128)} %bitcast.149, f32[240,3,768]{2,1,0:T(4,128)} %get-tuple-element.429, f32[]{:T(128)} %bitcast.150, f32[]{:T(128)} %bitcast.151, ...), kind=kLoop, calls=%fused_computation.10.clone.1 | loop fusion | flops 2764800 | bytes 4423716 | tf_op jit(solution)/shard_map/while/body/eval_jaxpr/add | solution.py:21
  91.7 13.1 %multiply_add_fusion.12 = (f32[240,1,768]{2,1,0:T(1,128)S(1)}, f32[240,1,768]{2,1,0:T(1,128)S(1)}, f32[240,1,768]{2,1,0:T(1,128)S(1)}) fusion(f32[]{:T(128)} %bitcast.147, f32[]{:T(128)} %bitcast.148, f32[]{:T(128)} %bitcast.149, f32[240,3,768]{2,1,0:T(4,128)} %get-tuple-element.429, f32[]{:T(128)} %bitcast.150, f32[]{:T(128)} %bitcast.151, ...), kind=kLoop, calls=%fused_computation.10.clone.1 | loop fusion | flops 2764800 | bytes 4423716 | tf_op jit(solution)/shard_map/while/body/eval_jaxpr/add | solution.py:21
  127.1 13.1 %multiply_add_fusion.12 = (f32[240,1,768]{2,1,0:T(1,128)S(1)}, f32[240,1,768]{2,1,0:T(1,128)S(1)}, f32[240,1,768]{2,1,0:T(1,128)S(1)}) fusion(f32[]{:T(128)} %bitcast.147, f32[]{:T(128)} %bitcast.148, f32[]{:T(128)} %bitcast.149, f32[240,3,768]{2,1,0:T(4,128)} %get-tuple-element.429, f32[]{:T(128)} %bitcast.150, f32[]{:T(128)} %bitcast.151, ...), kind=kLoop, calls=%fused_computation.10.clone.1 | loop fusion | flops 2764800 | bytes 4423716 | tf_op jit(solution)/shard_map/while/body/eval_jaxpr/add | solution.py:21
  162.4 13.1 %multiply_add_fusion.12 = (f32[240,1,768]{2,1,0:T(1,128)S(1)}, f32[240,1,768]{2,1,0:T(1,128)S(1)}, f32[240,1,768]{2,1,0:T(1,128)S(1)}) fusion(f32[]{:T(128)} %bitcast.147, f32[]{:T(128)} %bitcast.148, f32[]{:T(128)} %bitcast.149, f32[240,3,768]{2,1,0:T(4,128)} %get-tuple-element.429, f32[]{:T(128)} %bitcast.150, f32[]{:T(128)} %bitcast.151, ...), kind=kLoop, calls=%fused_computation.10.clone.1 | loop fusion | flops 2764800 | bytes 4423716 | tf_op jit(solution)/shard_map/while/body/eval_jaxpr/add | solution.py:21
  197.7 13.1 %multiply_add_fusion.12 = (f32[240,1,768]{2,1,0:T(1,128)S(1)}, f32[240,1,768]{2,1,0:T(1,128)S(1)}, f32[240,1,768]{2,1,0:T(1,128)S(1)}) fusion(f32[]{:T(128)} %bitcast.147, f32[]{:T(128)} %bitcast.148, f32[]{:T(128)} %bitcast.149, f32[240,3,768]{2,1,0:T(4,128)} %get-tuple-element.429, f32[]{:T(128)} %bitcast.150, f32[]{:T(128)} %bitcast.151, ...), kind=kLoop, calls=%fused_computation.10.clone.1 | loop fusion | flops 2764800 | bytes 4423716 | tf_op jit(solution)/shard_map/while/body/eval_jaxpr/add | solution.py:21
  232.9 13.1 %multiply_add_fusion.12 = (f32[240,1,768]{2,1,0:T(1,128)S(1)}, f32[240,1,768]{2,1,0:T(1,128)S(1)}, f32[240,1,768]{2,1,0:T(1,128)S(1)}) fusion(f32[]{:T(128)} %bitcast.147, f32[]{:T(128)} %bitcast.148, f32[]{:T(128)} %bitcast.149, f32[240,3,768]{2,1,0:T(4,128)} %get-tuple-element.429, f32[]{:T(128)} %bitcast.150, f32[]{:T(128)} %bitcast.151, ...), kind=kLoop, calls=%fused_computation.10.clone.1 | loop fusion | flops 2764800 | bytes 4423716 | tf_op jit(solution)/shard_map/while/body/eval_jaxpr/add | solution.py:21
  268.2 13.1 %multiply_add_fusion.12 = (f32[240,1,768]{2,1,0:T(1,128)S(1)}, f32[240,1,768]{2,1,0:T(1,128)S(1)}, f32[240,1,768]{2,1,0:T(1,128)S(1)}) fusion(f32[]{:T(128)} %bitcast.147, f32[]{:T(128)} %bitcast.148, f32[]{:T(128)} %bitcast.149, f32[240,3,768]{2,1,0:T(4,128)} %get-tuple-element.429, f32[]{:T(128)} %bitcast.150, f32[]{:T(128)} %bitcast.151, ...), kind=kLoop, calls=%fused_computation.10.clone.1 | loop fusion | flops 2764800 | bytes 4423716 | tf_op jit(solution)/shard_map/while/body/eval_jaxpr/add | solution.py:21
  303.6 13.1 %multiply_add_fusion.12 = (f32[240,1,768]{2,1,0:T(1,128)S(1)}, f32[240,1,768]{2,1,0:T(1,128)S(1)}, f32[240,1,768]{2,1,0:T(1,128)S(1)}) fusion(f32[]{:T(128)} %bitcast.147, f32[]{:T(128)} %bitcast.148, f32[]{:T(128)} %bitcast.149, f32[240,3,768]{2,1,0:T(4,128)} %get-tuple-element.429, f32[]{:T(128)} %bitcast.150, f32[]{:T(128)} %bitcast.151, ...), kind=kLoop, calls=%fused_computation.10.clone.1 | loop fusion | flops 2764800 | bytes 4423716 | tf_op jit(solution)/shard_map/while/body/eval_jaxpr/add | solution.py:21
  339.0 13.1 %multiply_add_fusion.12 = (f32[240,1,768]{2,1,0:T(1,128)S(1)}, f32[240,1,768]{2,1,0:T(1,128)S(1)}, f32[240,1,768]{2,1,0:T(1,128)S(1)}) fusion(f32[]{:T(128)} %bitcast.147, f32[]{:T(128)} %bitcast.148, f32[]{:T(128)} %bitcast.149, f32[240,3,768]{2,1,0:T(4,128)} %get-tuple-element.429, f32[]{:T(128)} %bitcast.150, f32[]{:T(128)} %bitcast.151, ...), kind=kLoop, calls=%fused_computation.10.clone.1 | loop fusion | flops 2764800 | bytes 4423716 | tf_op jit(solution)/shard_map/while/body/eval_jaxpr/add | solution.py:21
  374.3 13.1 %multiply_add_fusion.12 = (f32[240,1,768]{2,1,0:T(1,128)S(1)}, f32[240,1,768]{2,1,0:T(1,128)S(1)}, f32[240,1,768]{2,1,0:T(1,128)S(1)}) fusion(f32[]{:T(128)} %bitcast.147, f32[]{:T(128)} %bitcast.148, f32[]{:T(128)} %bitcast.149, f32[240,3,768]{2,1,0:T(4,128)} %get-tuple-element.429, f32[]{:T(128)} %bitcast.150, f32[]{:T(128)} %bitcast.151, ...), kind=kLoop, calls=%fused_computation.10.clone.1 | loop fusion | flops 2764800 | bytes 4423716 | tf_op jit(solution)/shard_map/while/body/eval_jaxpr/add | solution.py:21
  409.6 13.1 %multiply_add_fusion.12 = (f32[240,1,768]{2,1,0:T(1,128)S(1)}, f32[240,1,768]{2,1,0:T(1,128)S(1)}, f32[240,1,768]{2,1,0:T(1,128)S(1)}) fusion(f32[]{:T(128)} %bitcast.147, f32[]{:T(128)} %bitcast.148, f32[]{:T(128)} %bitcast.149, f32[240,3,768]{2,1,0:T(4,128)} %get-tuple-element.429, f32[]{:T(128)} %bitcast.150, f32[]{:T(128)} %bitcast.151, ...), kind=kLoop, calls=%fused_computation.10.clone.1 | loop fusion | flops 2764800 | bytes 4423716 | tf_op jit(solution)/shard_map/while/body/eval_jaxpr/add | solution.py:21
  450.0 232.0 %while.30 = (s32[]{:T(128)}, f32[240,3,768]{2,1,0:T(4,128)S(1)}, bf16[12,240,3,768]{3,1,0,2:T(8,128)(2,1)}, f32[12,240,3,768]{3,2,1,0:T(4,128)}, f32[12,3,3]{2,1...) while((s32[]{:T(128)}, f32[240,3,768]{2,1,0:T(4,128)S(1)}, ...), condition=%wide.region_6.7_spmd.clone, body=%wide.region_5.6_spmd.clone.sunk | while | flops 7188484 | bytes 23224624 | solution.py:64
  688.4 34.7 %cosine_convert_fusion = (bf16[1,640,3072]{2,1,0:T(8,128)(2,1)S(1)}, bf16[1,640,3072]{2,1,0:T(8,128)(2,1)}) fusion(s32[640]{0:T(1024)S(1)} %copy-done.1), kind=kLoop, calls=%fused_computation.30 | loop fusion | flops 23592960 | bytes 7866880 | tf_op jit(solution)/shard_map/convert.2
  728.9 105.7 %all-to-all-done = bf16[240,36,768]{2,0,1:T(8,128)(2,1)} async-done(((bf16[240,36,768]{2,0,1:T(8,128)(2,1)}), bf16[240,36,768]{2,0,1:T(8,128)(2,1)}, u32[]{:S(2)}, u32[]{:S(2)}) %all-to-all-start) | async-done | bytes 13271072 | tf_op jit(solution)/shard_map/all_to_all | solution.py:93
  834.7 25.5 %copy.36 = bf16[240,9,4,768]{3,2,1,0:T(4,128)(2,1)S(1)} copy(bf16[240,9,4,768]{3,0,1,2:T(8,128)(2,1)} %bitcast.45) | data formatting | bytes 26542080 | tf_op jit(solution)/shard_map/all_to_all | solution.py:93
  871.7 19.1 %convolution_convert_fusion = bf16[1280,2160]{0,1:T(8,128)(2,1)} fusion(bf16[1280,3072]{1,0:T(8,128)(2,1)S(1)} %bitcast.186, bf16[2160,3072]{1,0:T(8,128)(2,1)S(1)} %bitcast.182), kind=kOutput, calls=%fused_computation.24 | convolution fusion | flops 16989696000 | bytes 26664960 | tf_op jit(solution)/shard_map/dot_general | solution.py:95
  902.2 20.1 %copy.37 = bf16[1,2,640,240,9]{3,1,4,0,2:T(2,128)(2,1)} copy(bf16[1,2,640,240,9]{2,1,4,3,0:T(2,128)(2,1)} %broadcast_in_dim_reshape.3) | data formatting | bytes 11059200 | tf_op jit(solution)/shard_map/broadcast_in_dim;reshape | solution.py:100
  922.3 14.1 %all-to-all-start.1 = ((bf16[1,2,640,240,9]{3,1,4,0,2:T(2,128)(2,1)}), bf16[1,2,640,240,9]{3,1,4,0,2:T(2,128)(2,1)}, u32[]{:S(2)}, u32[]{:S(2)}) async-start(bf16[1,2,640,240,9]{3,1,4,0,2:T(2,128)(2,1)} %copy.37), calls=%async_computation.1 | async-start | bytes 11796480 | tf_op jit(solution)/shard_map/all_to_all | solution.py:100
  937.0 130.7 %all-to-all-done.1 = bf16[1,2,640,240,9]{3,1,4,0,2:T(2,128)(2,1)} async-done(((bf16[1,2,640,240,9]{3,1,4,0,2:T(2,128)(2,1)}), bf16[1,2,640,240,9]{3,1,4,0,2:T(2,128)(2,1)}, u32[]{:S(2)}, u32[]{:S(2)}) %all-to-all-start.1) | async-done | bytes 5529632 | tf_op jit(solution)/shard_map/all_to_all | solution.py:100
  1087.6 13.8 %copy.39 = bf16[20,72,1920]{1,0,2:T(8,128)(2,1)} copy(bf16[20,72,1920]{2,1,0:T(8,128)(2,1)} %reshape.773) | data formatting | bytes 11059200 | tf_op jit(solution)/shard_map/reshape | solution.py:102
  1121.9 22.2 %broadcast_select_fusion.1 = f32[20,72,896]{2,1,0:T(8,128)} fusion(pred[20,896]{1,0:T(8,128)(4,1)S(1)} %add_compare_fusion, bf16[20,1280,896]{2,1,0:T(8,128)(2,1)} %param.17, bf16[20,72,1280]{1,0,2:T(8,128)(2,1)} %select_bitcast_fusion), kind=kOutput, calls=%fused_computation.38 | convolution fusion | flops 3304304640 | bytes 54740480 | tf_op jit(solution)/shard_map/scl,sln->scn/dot_general | solution.py:107
  (210 shorter events, 585.0 us)
Async XLA Ops:
  3.6 14.7 %copy-start = (f32[3,3,12]{2,1,0:T(4,128)S(1)}, f32[3,3,12]{2,1,0:T(4,128)}, u32[]{:S(2)}) copy-start(f32[3,3,12]{2,1,0:T(4,128)} %param.14) | copy-start | bytes 1300
  682.0 6.4 copy-start.1
  682.0 152.7 %all-to-all-start = ((bf16[240,36,768]{2,0,1:T(8,128)(2,1)}), bf16[240,36,768]{2,0,1:T(8,128)(2,1)}, u32[]{:S(2)}, u32[]{:S(2)}) async-start(bf16[240,36,768]{2,0,1:T(8,128)(2,1)} %bitcast.179), calls=%async_computation | async-start | bytes 26542080 | tf_op jit(solution)/shard_map/all_to_all | solution.py:93
  834.7 37.0 %slice-start = ((s8[7864320]{0:T(1024)(128)(4,1)}), s8[4194304]{0:T(1024)(128)(4,1)S(1)}, s32[]{:S(2)}) async-start(s8[7864320]{0:T(1024)(128)(4,1)} %bitcast.184), calls=%async_computation.2 | async-start | bytes 8388608
  860.1 11.6 %slice-start.1 = ((s8[7864320]{0:T(1024)(128)(4,1)}), s8[3670016]{0:T(1024)(128)(4,1)S(1)}, s32[]{:S(2)}) async-start(s8[7864320]{0:T(1024)(128)(4,1)} %bitcast.184), calls=%async_computation.3 | async-start | bytes 7340032
  922.3 14.1 %copy-start.2 = (s32[8]{0:T(128)S(1)}, s32[8]{0:T(128)}, u32[]{:S(2)}) copy-start(s32[8]{0:T(128)} %param.12) | copy-start | bytes 100
  922.3 145.5 %all-to-all-start.1 = ((bf16[1,2,640,240,9]{3,1,4,0,2:T(2,128)(2,1)}), bf16[1,2,640,240,9]{3,1,4,0,2:T(2,128)(2,1)}, u32[]{:S(2)}, u32[]{:S(2)}) async-start(bf16[1,2,640,240,9]{3,1,4,0,2:T(2,128)(2,1)} %copy.37), calls=%async_computation.1 | async-start | bytes 11796480 | tf_op jit(solution)/shard_map/all_to_all | solution.py:100
where the time goes:
time: 1160 us; the launch traced here: 1140 us
  other arithmetic  662 us (57%)
  waiting for transfers between devices  236 us (20%)
  local copies, waits for them, and re-layouts  182 us (16%)
  matrix products  41.3 us (4%)
  starting transfers between devices  20.5 us (2%)
    add x36, other arithmetic, apply_block(): total = total + block[row_index, col_index] * vector[:, col_index]  381 us
    all_to_all x1, waiting for transfers between devices, shards(): lax.all_to_all(fourier[None], ('aa', 'ba'), split_axis=2, concat_axis=0,...  131 us
    all_to_all x1, waiting for transfers between devices, shards(): lax.all_to_all(smooth, 'ba', split_axis=1, concat_axis=2, tiled=True)  106 us
    sub x24, other arithmetic, backward(): result = sweep - apply_block(coupling_lev, carry)  90.3 us
    sub x12, other arithmetic, forward(): sweep = apply_block(inverse_lev, source - apply_block(lower_lev, carry))  70.2 us
    dynamic_update_slice x12, other arithmetic, diffuse(): lax.scan(forward, zero_state, (values, lower_seq, inverse_seq))  46.4 us
    another operation x3, other arithmetic  34.8 us
    another operation x2, local copies, waits for them, and re-layouts, shards(): fourier[None]  31.5 us
  transfers between devices with their start and end apart: 2, of which 2 were waited for; matrix products, arithmetic and copies ran while one was open for 4% of the time, Pallas kernels for 0%

commit v1 on v0

v1 whole, which is shorter than its diff:
```python
import functools
import math

import jax
import jax.numpy as jnp
import numpy as np
from jax import lax
from jax.experimental import pallas as pl
from jax.experimental.pallas import tpu as pltpu
from jax.sharding import PartitionSpec as P

NT = 1279
CHUNKS = 6
VMEM = 48 * 1024 * 1024


def params():
    return pltpu.CompilerParams(vmem_limit_bytes=VMEM)


def angle(phase, lon_total):
    return phase.astype(jnp.float32) * (2.0 * math.pi / lon_total)


def table_kernel(base_ref, step_ref, out_ref, *, lon_total):
    base = angle(base_ref[...], lon_total)
    step = angle(step_ref[...], lon_total)
    cos_a, sin_a = jnp.cos(base), jnp.sin(base)
    cos_b, sin_b = jnp.cos(step), jnp.sin(step)
    for block in range(out_ref.shape[1] // 128):
        one = slice(block, block + 1)
        out_ref[:, block * 128:(block + 1) * 128] = (
            cos_a[:, one] * cos_b - sin_a[:, one] * sin_b
        ).astype(jnp.bfloat16)


def make_table(waves, quadrant, first_lon, lon_count, lon_total):
    rows = waves.shape[0]
    blocks = lon_count // 128
    starts = first_lon + 128 * jnp.arange(128, dtype=jnp.int32)
    base = (waves[:, None] * starts[None, :] + quadrant[:, None] * (lon_total // 4)) % lon_total
    step = (waves[:, None] * jnp.arange(128, dtype=jnp.int32)[None, :]) % lon_total
    tile = rows // 8 if rows % 64 == 0 else rows
    return pl.pallas_call(
        functools.partial(table_kernel, lon_total=lon_total),
        grid=(rows // tile,),
        in_specs=[pl.BlockSpec((tile, 128), lambda i: (i, 0))] * 2,
        out_specs=pl.BlockSpec((tile, blocks * 128), lambda i: (i, 0)),
        out_shape=jax.ShapeDtypeStruct((rows, blocks * 128), jnp.bfloat16),
        compiler_params=params(),
        name="table",
    )(base, step)


NN = (((1,), (1,)), ((), ()))


def dft_kernel(table_ref, grid_ref, *rest):
    out_ref = rest[-1]
    width = grid_ref.shape[3]
    dests, _, rows, _ = out_ref.shape
    total = lax.dot_general(table_ref[:, :width], grid_ref[0, 0], NN, preferred_element_type=jnp.float32)
    total += lax.dot_general(table_ref[:, width:], grid_ref[1, 0], NN, preferred_element_type=jnp.float32)
    for dest in range(dests):
        piece = total[dest * rows:(dest + 1) * rows]
        if len(rest) == 2:
            piece = piece + rest[0][dest, 0].astype(jnp.float32)
        out_ref[dest, 0] = piece.astype(jnp.bfloat16)


def dft(table, grid, first, count, dests, more=None):
    rows = table.shape[0] // dests
    slots = grid.shape[2]
    out_spec = pl.BlockSpec((dests, 1, rows, slots), lambda i: (0, i, 0, 0))
    in_specs = [
        pl.BlockSpec(table.shape, lambda i: (0, 0)),
        pl.BlockSpec((2, 1) + grid.shape[2:], lambda i: (0, first + i, 0, 0)),
    ]
    operands = [table, grid]
    if more is not None:
        in_specs.append(out_spec)
        operands.append(more)
    flops = 2 * table.shape[0] * table.shape[1] * slots * count
    return pl.pallas_call(
        dft_kernel,
        grid=(count,),
        in_specs=in_specs,
        out_specs=out_spec,
        out_shape=jax.ShapeDtypeStruct((dests, count, rows, slots), jnp.bfloat16),
        compiler_params=params(),
        cost_estimate=pl.CostEstimate(flops=flops, bytes_accessed=table.size * 2 + count * slots * 6000, transcendentals=0),
        name="dft",
    )(*operands)


def place_kernel(place_ref, in_ref, out_ref):
    bands, _, count, rows, slots = in_ref.shape
    for q in range(count):
        total = jnp.dot(in_ref[0, 0, q], place_ref[0], preferred_element_type=jnp.float32)
        for band in range(1, bands):
            total += jnp.dot(in_ref[band, 0, q], place_ref[band], preferred_element_type=jnp.float32)
        out_ref[0, q] = total.astype(jnp.bfloat16)


def place_rows(place, arrived):
    bands, pair, count, rows, slots = arrived.shape
    lats = place.shape[2]
    flops = 2 * pair * count * rows * bands * slots * lats
    return pl.pallas_call(
        place_kernel,
        grid=(pair,),
        in_specs=[
            pl.BlockSpec(place.shape, lambda i: (0, 0, 0)),
            pl.BlockSpec((bands, 1, count, rows, slots), lambda i: (0, i, 0, 0, 0)),
        ],
        out_specs=pl.BlockSpec((1, count, rows, lats), lambda i: (i, 0, 0, 0)),
        out_shape=jax.ShapeDtypeStruct((pair, count, rows, lats), jnp.bfloat16),
        compiler_params=params(),
        cost_estimate=pl.CostEstimate(flops=flops, bytes_accessed=place.size * 2, transcendentals=0),
        name="place",
    )(place, arrived)


def solve_kernel(lower_ref, inverse_ref, upper_ref, out_ref, *, fields, levels):
    lane = lax.broadcasted_iota(jnp.int32, (1, 128), 1)
    cut = lambda ref, a, b, k: ref[(a * fields + b) * levels + k]

    def apply(ref, k, vector):
        return [sum(cut(ref, a, b, k) * vector[b] for b in range(fields)) for a in range(fields)]

    state = [jnp.zeros((1, 128), jnp.float32) for _ in range(fields)]
    sweeps = []
    for k in range(levels):
        low = apply(lower_ref, k, state)
        source = [(lane == f * levels + k).astype(jnp.float32) - low[f] for f in range(fields)]
        state = apply(inverse_ref, k, source)
        sweeps.append(state)
    state = [jnp.zeros((1, 128), jnp.float32) for _ in range(fields)]
    for k in range(levels - 1, -1, -1):
        back = apply(inverse_ref, k, apply(upper_ref, k, state))
        state = [sweeps[k][f] - back[f] for f in range(fields)]
        for f in range(fields):
            out_ref[f * levels + k:f * levels + k + 1, :] = state[f]


def vertical_operator(lower_blocks, pivot_inverse, upper_blocks):
    fields, _, levels = lower_blocks.shape
    whole = pl.pallas_call(
        functools.partial(solve_kernel, fields=fields, levels=levels),
        in_specs=[pl.BlockSpec(memory_space=pltpu.SMEM)] * 3,
        out_specs=pl.BlockSpec(memory_space=pltpu.VMEM),
        out_shape=jax.ShapeDtypeStruct((fields * levels, 128), jnp.float32),
        name="vertical",
    )(lower_blocks.reshape(-1), pivot_inverse.reshape(-1), upper_blocks.reshape(-1))
    return whole[:, :fields * levels]


def legendre_kernel(owner_ref, mix_ref, panel_ref, legendre_ref, out_ref):
    slot = pl.program_id(0)
    total = jnp.dot(panel_ref[0], legendre_ref[0], preferred_element_type=jnp.float32)
    high = total.astype(jnp.bfloat16)
    low = (total - high.astype(jnp.float32)).astype(jnp.bfloat16)
    count = total.shape[0]
    mixed = jnp.dot(mix_ref[0], high, preferred_element_type=jnp.float32)
    mixed += jnp.dot(mix_ref[0], low, preferred_element_type=jnp.float32)
    mixed += jnp.dot(mix_ref[1], high, preferred_element_type=jnp.float32)
    degree = lax.broadcasted_iota(jnp.int32, mixed.shape, 1)
    out_ref[0] = jnp.where(degree + owner_ref[slot] <= NT, mixed, 0.0)


def project(owners, mix, panels, legendre):
    slots, rows, lats = panels.shape
    degrees = legendre.shape[2]
    return pl.pallas_call(
        legendre_kernel,
        grid=(slots,),
        in_specs=[
            pl.BlockSpec(memory_space=pltpu.SMEM),
            pl.BlockSpec(mix.shape, lambda i: (0, 0, 0)),
            pl.BlockSpec((1, rows, lats), lambda i: (i, 0, 0)),
            pl.BlockSpec((1, lats, degrees), lambda i: (i, 0, 0)),
        ],
        out_specs=pl.BlockSpec((1, rows, degrees), lambda i: (i, 0, 0)),
        out_shape=jax.ShapeDtypeStruct((slots, rows, degrees), jnp.float32),
        compiler_params=params(),
        name="legendre",
    )(owners, mix, panels, legendre)


def shards(bands, pairs, grid_fields, band_rows, wave_owner, lower_blocks, pivot_inverse, upper_blocks, legendre):
    slot_rows, columns, lons = grid_fields.shape
    lon_total = lons * 2 * pairs
    per, lats, _ = legendre.shape
    a, b = lax.axis_index("aa"), lax.axis_index("ba")
    side = b // 2
    half = columns // 2
    group = 2 * pairs

    grid = jnp.transpose(grid_fields, (1, 0, 2)).reshape(2, half, slot_rows, lons)
    duos = [[2 * y, 2 * y + 1] for y in range(pairs)]
    grid = lax.all_to_all(grid, "ba", split_axis=0, concat_axis=0, axis_index_groups=duos, tiled=True)

    owners = wave_owner.reshape(bands, pairs, 2, per)
    pad = -(2 * per) % 8
    rows = 2 * per + pad

    def side_rows(which):
        mine = lax.dynamic_index_in_dim(owners, which, 1, keepdims=False)
        waves = jnp.concatenate([mine, mine], axis=2)
        return jnp.pad(waves, ((0, 0), (0, 0), (0, pad))).reshape(-1)

    quadrant = jnp.asarray(np.tile(np.repeat(np.arange(2), per).tolist() + [0] * pad, bands * 2), jnp.int32)
    tables = [make_table(side_rows(w), quadrant, side * 2 * lons, 2 * lons, lon_total) for w in (1 - side, side)]

    ends = jnp.cumsum(band_rows)
    slot = jnp.arange(slot_rows, dtype=jnp.int32)
    target = jnp.where(slot[None, :] < band_rows[:, None], (ends - band_rows)[:, None] + slot[None, :], -1)
    place = (target[:, :, None] == jnp.arange(lats, dtype=jnp.int32)).astype(jnp.bfloat16)

    dests = 2 * bands
    count = half // CHUNKS
    across = [(2 * y + c, 2 * (1 - y) + c) for y in range(2) for c in range(2)]
    teams = [[aa * group + 2 * y + c for aa in range(bands) for c in range(2)] for y in range(pairs)]
    sent = []
    for chunk in range(CHUNKS):
        part = dft(tables[0], grid, chunk * count, count, dests)
        sent.append(lax.ppermute(part, "ba", across))
    placed = []
    for chunk in range(CHUNKS):
        full = dft(tables[1], grid, chunk * count, count, dests, sent[chunk])
        arrived = lax.all_to_all(full, ("aa", "ba"), split_axis=0, concat_axis=0, axis_index_groups=teams, tiled=True)
        placed.append(place_rows(place, arrived.reshape(bands, 2, count, rows, slot_rows)))
    panels = jnp.stack(placed, axis=1)[:, :, :, :2 * per].reshape(columns, 2, per, lats)
    panels = jnp.transpose(panels, (2, 1, 0, 3)).reshape(per, 2 * columns, lats)

    operator = vertical_operator(lower_blocks, pivot_inverse, upper_blocks)
    mix = jnp.kron(jnp.eye(2, dtype=jnp.float32), operator)
    high = mix.astype(jnp.bfloat16)
    low = (mix - high.astype(jnp.float32)).astype(jnp.bfloat16)
    mine = lax.dynamic_slice_in_dim(wave_owner, (a * group + b) * per, per)
    return project(mine, jnp.stack([high, low]), panels, legendre)


def solution(mesh):
    bands, group = mesh.shape["aa"], mesh.shape["ba"]
    placed = (P("aa", None, "ba"), P(), P(), P(), P(), P(), P(("aa", "ba"), None, None))
    return jax.shard_map(
        functools.partial(shards, bands, group // 2),
        mesh=mesh, in_specs=placed, out_specs=P(("aa", "ba"), None, None), check_vma=False,
    )
```

time: 1160 us -> 367 us (0.32); the launches traced: 1140 us -> 365 us
  other arithmetic: 662 us -> 5.81 us
  local copies, waits for them, and re-layouts: 182 us -> 40.9 us
  Pallas kernels: 0 us -> 132 us
  waiting for transfers between devices: 236 us -> 131 us
  matrix products: 41.3 us -> 0 us
  starting transfers between devices: 20.5 us -> 54.6 us
    add x39 -> x1, other arithmetic: 383 us -> 0.01 us  [make_table(): starts = first_lon + 128 * jnp.arange(128, dtype=jnp.int32)]
    all_to_all x2 -> x7, waiting for transfers between devices: 236 us -> 4.67 us  [the longest x1 4.65 us: shards(): lax.all_to_all(grid, 'ba', split_axis=0, concat_axis=0, axis_index_groups...]
    sub x37 -> x1, other arithmetic: 160 us -> 0.01 us  [shards(): ends - band_rows]
    pallas_call x0 -> x22, Pallas kernels: none -> 132 us  [the longest x6 47.9 us: place_rows(): pl.pallas_call(place_kernel, grid=(pair,), in_specs=[pl.BlockSpec(place.s...]
    ppermute x0 -> x6, waiting for transfers between devices: none -> 126 us  [shards(): sent.append(lax.ppermute(part, 'ba', across))]
    dynamic_update_slice x12 -> x0, other arithmetic: 46.4 us -> none  [diffuse(): lax.scan(forward, zero_state, (values, lower_seq, inverse_seq))]
    dot_general x2 -> x0, matrix products: 41.3 us -> none  [the longest x1 22.2 us: shards(): jnp.einsum('scl,sln->scn', panels, legendre, preferred_element_type=jnp.f...]
    another operation x6 -> x2, other arithmetic: 40.7 us -> 0.19 us
  transfers between devices with their start and end apart: 2 -> 13, of which waited for: 2 -> 7; matrix products, arithmetic and copies ran while one was open for 4% -> 2% of each run, Pallas kernels for 0% -> 24%
where the time goes in v1:
time: 367 us; the launch traced here: 365 us
  Pallas kernels  132 us (36%)
  waiting for transfers between devices  131 us (36%)
  starting transfers between devices  54.6 us (15%)
  local copies, waits for them, and re-layouts  40.9 us (11%)
  other arithmetic  5.81 us (2%)
    ppermute x6, waiting for transfers between devices, shards(): sent.append(lax.ppermute(part, 'ba', across))  126 us
    pallas_call x6, Pallas kernels, place_rows(): pl.pallas_call(place_kernel, grid=(pair,), in_specs=[pl.BlockSpec(place.s...  47.9 us
    pallas_call x12, Pallas kernels, dft(): pl.pallas_call(dft_kernel, grid=(count,), in_specs=in_specs, out_specs=ou...  45.4 us
    all_to_all x6, starting transfers between devices, shards(): lax.all_to_all(full, ('aa', 'ba'), split_axis=0, concat_axis=0, axis_inde...  35 us
    pallas_call x1, Pallas kernels, project(): pl.pallas_call(legendre_kernel, grid=(slots,), in_specs=[pl.BlockSpec(mem...  28.8 us
    unnamed x57, local copies, waits for them, and re-layouts  18.2 us
    ppermute x6, starting transfers between devices, shards(): sent.append(lax.ppermute(part, 'ba', across))  10.9 us
    pallas_call x2, Pallas kernels, make_table(): pl.pallas_call(functools.partial(table_kernel, lon_total=lon_total), grid...  8.74 us
  transfers between devices with their start and end apart: 13, of which 7 were waited for; matrix products, arithmetic and copies ran while one was open for 2% of the time, Pallas kernels for 24%

profile of v1, /device:TPU:0, one launch (start us, length us, event | category | flops | bytes accessed | tf_op | source)
XLA Modules:
  0.0 364.9 jit_solution(4197611651754289781)
XLA Ops:
  0.0 8.7 %all-to-all-start = ((bf16[2,18,240,768]{3,2,1,0:T(8,128)(2,1)}), bf16[2,18,240,768]{3,2,1,0:T(8,128)(2,1)}, u32[]{:S(2)}, u32[]{:S(2)}) async-start(bf16[2,18,240,768]{3,2,1,0:T(8,128)(2,1)} %bitcast.35), calls=%async_computation | async-start | bytes 26542080 | tf_op jit(solution)/shard_map/all_to_all | solution.py:201
  15.1 4.7 %all-to-all-done.grid_ref = bf16[2,18,240,768]{3,2,1,0:T(8,128)(2,1)} async-done(((bf16[2,18,240,768]{3,2,1,0:T(8,128)(2,1)}), bf16[2,18,240,768]{3,2,1,0:T(8,128)(2,1)}, u32[]{:S(2)}, u32[]{:S(2)}) %all-to-all-start) | async-done | bytes 13271072 | tf_op jit(solution)/shard_map/all_to_all | solution.py:201
  30.9 17.7 %collective-permute-done.1.rest_0_ = bf16[16,3,40,240]{3,2,1,0:T(8,128)(2,1)S(1)} collective-permute-done((bf16[16,3,40,240]{3,2,1,0:T(8,128)(2,1)S(1)}, bf16[16,3,40,240]{3,2,1,0:T(8,128)(2,1)S(1)}, u32[]{:S(2)}, u32[]{:S(2)}) %collective-permute-start.1) | collective-permute-done | bytes 921632 | tf_op jit(solution)/shard_map/ppermute | solution.py:227
  53.2 6.1 %all-to-all-start.2 = ((bf16[16,3,40,240]{3,2,1,0:T(8,128)(2,1)}), bf16[16,3,40,240]{3,2,1,0:T(8,128)(2,1)S(1)}, u32[]{:S(2)}, u32[]{:S(2)}) async-start(bf16[16,3,40,240]{3,2,1,0:T(8,128)(2,1)} %copy-done.12), calls=%async_computation.2 | async-start | bytes 1966080 | tf_op jit(solution)/shard_map/all_to_all | solution.py:231
  66.2 22.6 %collective-permute-done.2.rest_0_ = bf16[16,3,40,240]{3,2,1,0:T(8,128)(2,1)S(1)} collective-permute-done((bf16[16,3,40,240]{3,2,1,0:T(8,128)(2,1)S(1)}, bf16[16,3,40,240]{3,2,1,0:T(8,128)(2,1)S(1)}, u32[]{:S(2)}, u32[]{:S(2)}) %collective-permute-start.2) | collective-permute-done | bytes 921632 | tf_op jit(solution)/shard_map/ppermute | solution.py:227
  93.4 5.8 %all-to-all-start.3 = ((bf16[16,3,40,240]{3,2,1,0:T(8,128)(2,1)}), bf16[16,3,40,240]{3,2,1,0:T(8,128)(2,1)}, u32[]{:S(2)}, u32[]{:S(2)}) async-start(bf16[16,3,40,240]{3,2,1,0:T(8,128)(2,1)} %copy-done.9), calls=%async_computation.3 | async-start | bytes 1966080 | tf_op jit(solution)/shard_map/all_to_all | solution.py:231
  106.0 22.5 %collective-permute-done.3.rest_0_ = bf16[16,3,40,240]{3,2,1,0:T(8,128)(2,1)S(1)} collective-permute-done((bf16[16,3,40,240]{3,2,1,0:T(8,128)(2,1)S(1)}, bf16[16,3,40,240]{3,2,1,0:T(8,128)(2,1)S(1)}, u32[]{:S(2)}, u32[]{:S(2)}) %collective-permute-start.3) | collective-permute-done | bytes 921632 | tf_op jit(solution)/shard_map/ppermute | solution.py:227
  133.2 5.8 %all-to-all-start.4 = ((bf16[16,3,40,240]{3,2,1,0:T(8,128)(2,1)}), bf16[16,3,40,240]{3,2,1,0:T(8,128)(2,1)}, u32[]{:S(2)}, u32[]{:S(2)}) async-start(bf16[16,3,40,240]{3,2,1,0:T(8,128)(2,1)} %copy-done.10), calls=%async_computation.4 | async-start | bytes 1966080 | tf_op jit(solution)/shard_map/all_to_all | solution.py:231
  145.9 22.5 %collective-permute-done.4.rest_0_ = bf16[16,3,40,240]{3,2,1,0:T(8,128)(2,1)S(1)} collective-permute-done((bf16[16,3,40,240]{3,2,1,0:T(8,128)(2,1)S(1)}, bf16[16,3,40,240]{3,2,1,0:T(8,128)(2,1)S(1)}, u32[]{:S(2)}, u32[]{:S(2)}) %collective-permute-start.4) | collective-permute-done | bytes 921632 | tf_op jit(solution)/shard_map/ppermute | solution.py:227
  173.1 5.8 %all-to-all-start.5 = ((bf16[16,3,40,240]{3,2,1,0:T(8,128)(2,1)}), bf16[16,3,40,240]{3,2,1,0:T(8,128)(2,1)}, u32[]{:S(2)}, u32[]{:S(2)}) async-start(bf16[16,3,40,240]{3,2,1,0:T(8,128)(2,1)} %copy-done.11), calls=%async_computation.5 | async-start | bytes 1966080 | tf_op jit(solution)/shard_map/all_to_all | solution.py:231
  185.7 22.5 %collective-permute-done.5.rest_0_ = bf16[16,3,40,240]{3,2,1,0:T(8,128)(2,1)S(1)} collective-permute-done((bf16[16,3,40,240]{3,2,1,0:T(8,128)(2,1)S(1)}, bf16[16,3,40,240]{3,2,1,0:T(8,128)(2,1)S(1)}, u32[]{:S(2)}, u32[]{:S(2)}) %collective-permute-start.5) | collective-permute-done | bytes 921632 | tf_op jit(solution)/shard_map/ppermute | solution.py:227
  212.9 5.8 %all-to-all-start.6 = ((bf16[16,3,40,240]{3,2,1,0:T(8,128)(2,1)}), bf16[16,3,40,240]{3,2,1,0:T(8,128)(2,1)}, u32[]{:S(2)}, u32[]{:S(2)}) async-start(bf16[16,3,40,240]{3,2,1,0:T(8,128)(2,1)} %copy-done.7), calls=%async_computation.6 | async-start | bytes 1966080 | tf_op jit(solution)/shard_map/all_to_all | solution.py:231
  230.8 18.3 %collective-permute-done.rest_0_ = bf16[16,3,40,240]{3,2,1,0:T(8,128)(2,1)} collective-permute-done((bf16[16,3,40,240]{3,2,1,0:T(8,128)(2,1)}, bf16[16,3,40,240]{3,2,1,0:T(8,128)(2,1)}, u32[]{:S(2)}, u32[]{:S(2)}) %collective-permute-start) | collective-permute-done | bytes 921632 | tf_op jit(solution)/shard_map/ppermute | solution.py:227
  254.0 5.7 %all-to-all-start.1 = ((bf16[16,3,40,240]{3,2,1,0:T(8,128)(2,1)}), bf16[16,3,40,240]{3,2,1,0:T(8,128)(2,1)S(1)}, u32[]{:S(2)}, u32[]{:S(2)}) async-start(bf16[16,3,40,240]{3,2,1,0:T(8,128)(2,1)} %copy-done.8), calls=%async_computation.1 | async-start | bytes 1966080 | tf_op jit(solution)/shard_map/all_to_all | solution.py:231
  262.9 8.0 %place.11 = bf16[2,3,40,1280]{3,2,1,0:T(8,128)(2,1)S(1)} custom-call(bf16[8,240,1280]{2,1,0:T(8,128)(2,1)} %fusion.place_ref, bf16[8,2,3,40,240]{4,3,2,1,0:T(8,128)(2,1)} %bitcast.16.in_ref), custom_call_target="tpu_custom_call" | custom-call | flops 1179648000 | bytes 4915200 | tf_op jit(solution)/shard_map/place/pallas_call | solution.py:109
  270.9 8.0 %place.10 = bf16[2,3,40,1280]{3,2,1,0:T(8,128)(2,1)S(1)} custom-call(bf16[8,240,1280]{2,1,0:T(8,128)(2,1)} %fusion.place_ref, bf16[8,2,3,40,240]{4,3,2,1,0:T(8,128)(2,1)} %bitcast.14.in_ref), custom_call_target="tpu_custom_call" | custom-call | flops 1179648000 | bytes 4915200 | tf_op jit(solution)/shard_map/place/pallas_call | solution.py:109
  278.9 8.0 %place.9 = bf16[2,3,40,1280]{3,2,1,0:T(8,128)(2,1)S(1)} custom-call(bf16[8,240,1280]{2,1,0:T(8,128)(2,1)} %fusion.place_ref, bf16[8,2,3,40,240]{4,3,2,1,0:T(8,128)(2,1)} %bitcast.12.in_ref), custom_call_target="tpu_custom_call" | custom-call | flops 1179648000 | bytes 4915200 | tf_op jit(solution)/shard_map/place/pallas_call | solution.py:109
  287.7 8.0 %place.8 = bf16[2,3,40,1280]{3,2,1,0:T(8,128)(2,1)S(1)} custom-call(bf16[8,240,1280]{2,1,0:T(8,128)(2,1)} %fusion.place_ref, bf16[8,2,3,40,240]{4,3,2,1,0:T(8,128)(2,1)} %bitcast.10.in_ref), custom_call_target="tpu_custom_call" | custom-call | flops 1179648000 | bytes 4915200 | tf_op jit(solution)/shard_map/place/pallas_call | solution.py:109
  296.5 7.8 %place.7 = bf16[2,3,40,1280]{3,2,1,0:T(8,128)(2,1)S(1)} custom-call(bf16[8,240,1280]{2,1,0:T(8,128)(2,1)} %fusion.place_ref, bf16[8,2,3,40,240]{4,3,2,1,0:T(8,128)(2,1)S(1)} %bitcast.32), custom_call_target="tpu_custom_call" | custom-call | flops 1179648000 | bytes 4915200 | tf_op jit(solution)/shard_map/place/pallas_call | solution.py:109
  305.2 8.2 %place.6 = bf16[2,3,40,1280]{3,2,1,0:T(8,128)(2,1)S(1)} custom-call(bf16[8,240,1280]{2,1,0:T(8,128)(2,1)} %fusion.place_ref, bf16[8,2,3,40,240]{4,3,2,1,0:T(8,128)(2,1)S(1)} %bitcast.33), custom_call_target="tpu_custom_call" | custom-call | flops 1179648000 | bytes 4915200 | tf_op jit(solution)/shard_map/place/pallas_call | solution.py:109
  315.8 6.5 %reshape.181 = bf16[36,2,20,1280]{3,2,1,0:T(8,128)(2,1)} reshape(bf16[2,6,3,40,1280]{4,3,2,1,0:T(8,128)(2,1)} %copy.9) | data formatting | bytes 7372800 | tf_op jit(solution)/shard_map/reshape | solution.py:233
  322.3 5.4 %copy.10 = bf16[20,2,36,1280]{3,2,1,0:T(8,128)(2,1)} copy(bf16[20,2,36,1280]{3,0,1,2:T(8,128)(2,1)} %bitcast.34) | data formatting | bytes 7372800 | tf_op jit(solution)/shard_map/transpose | solution.py:234
  327.7 6.3 %reshape.182.panel_ref = bf16[20,72,1280]{2,1,0:T(8,128)(2,1)} reshape(bf16[20,2,36,1280]{3,2,1,0:T(8,128)(2,1)} %copy.10) | data formatting | bytes 7372800 | tf_op jit(solution)/shard_map/reshape | solution.py:234
  336.1 28.8 %legendre.1 = f32[20,72,896]{2,1,0:T(8,128)} custom-call(s32[20]{0:T(128)S(1)} %dynamic_slice.10.owner_ref, bf16[2,72,72]{2,1,0:T(8,128)(2,1)S(1)} %pad_maximum_fusion.mix_ref, bf16[20,72,1280]{2,1,0:T(8,128)(2,1)S(1)} %copy-done.6, bf16[20,1280,896]{2,1,0:T(8,128)(2,1)} %legendre_ref.1), custom_call_target="tpu_custom_call" | custom-call | tf_op jit(solution)/shard_map/legendre/pallas_call | solution.py:174
  (106 shorter events, 94.9 us)
Async XLA Ops:
  0.0 8.8 %copy-start.24 = (s32[640]{0:T(1024)S(1)}, s32[640]{0:T(1024)}, u32[]{:S(2)}) copy-start(s32[640]{0:T(1024)} %param.10) | copy-start | bytes 7684
  0.0 9.2 %copy-start.23 = (s32[640]{0:T(1024)S(1)}, s32[640]{0:T(1024)}, u32[]{:S(2)}) copy-start(s32[640]{0:T(1024)} %constant.75) | copy-start | bytes 7684
  0.0 19.7 %all-to-all-start = ((bf16[2,18,240,768]{3,2,1,0:T(8,128)(2,1)}), bf16[2,18,240,768]{3,2,1,0:T(8,128)(2,1)}, u32[]{:S(2)}, u32[]{:S(2)}) async-start(bf16[2,18,240,768]{3,2,1,0:T(8,128)(2,1)} %bitcast.35), calls=%async_computation | async-start | bytes 26542080 | tf_op jit(solution)/shard_map/all_to_all | solution.py:201
  15.1 8.4 %copy-start = (bf16[640,1536]{1,0:T(8,128)(2,1)}, bf16[640,1536]{1,0:T(8,128)(2,1)S(1)}, u32[]{:S(2)}) copy-start(bf16[640,1536]{1,0:T(8,128)(2,1)S(1)} %table.3.table_ref) | copy-start | bytes 5898244
  19.8 6.7 %copy-start.19 = (s32[640,128]{1,0:T(8,128)S(1)}, s32[640,128]{1,0:T(8,128)}, u32[]{:S(2)}) copy-start(s32[640,128]{1,0:T(8,128)} %get-tuple-element.11.step_ref) | copy-start | bytes 983044
  23.5 25.0 %collective-permute-start.1 = (bf16[16,3,40,240]{3,2,1,0:T(8,128)(2,1)S(1)}, bf16[16,3,40,240]{3,2,1,0:T(8,128)(2,1)S(1)}, u32[]{:S(2)}, u32[]{:S(2)}) collective-permute-start(bf16[16,3,40,240]{3,2,1,0:T(8,128)(2,1)S(1)} %dft.14), channel_id=1, source_target_pairs={{0,2},{1,3},{2,0},{3,1},{4,6},{5,7},{6,4},{7,5},{8,10},{9,11},{10,... | collective-permute-start | bytes 2764808 | tf_op jit(solution)/shard_map/ppermute | solution.py:227
  53.2 40.2 %all-to-all-start.2 = ((bf16[16,3,40,240]{3,2,1,0:T(8,128)(2,1)}), bf16[16,3,40,240]{3,2,1,0:T(8,128)(2,1)S(1)}, u32[]{:S(2)}, u32[]{:S(2)}) async-start(bf16[16,3,40,240]{3,2,1,0:T(8,128)(2,1)} %copy-done.12), calls=%async_computation.2 | async-start | bytes 1966080 | tf_op jit(solution)/shard_map/all_to_all | solution.py:231
  64.6 24.2 %collective-permute-start.2 = (bf16[16,3,40,240]{3,2,1,0:T(8,128)(2,1)S(1)}, bf16[16,3,40,240]{3,2,1,0:T(8,128)(2,1)S(1)}, u32[]{:S(2)}, u32[]{:S(2)}) collective-permute-start(bf16[16,3,40,240]{3,2,1,0:T(8,128)(2,1)S(1)} %dft.16), channel_id=1, source_target_pairs={{0,2},{1,3},{2,0},{3,1},{4,6},{5,7},{6,4},{7,5},{8,10},{9,11},{10,... | collective-permute-start | bytes 2764808 | tf_op jit(solution)/shard_map/ppermute | solution.py:227
  93.4 39.8 %all-to-all-start.3 = ((bf16[16,3,40,240]{3,2,1,0:T(8,128)(2,1)}), bf16[16,3,40,240]{3,2,1,0:T(8,128)(2,1)}, u32[]{:S(2)}, u32[]{:S(2)}) async-start(bf16[16,3,40,240]{3,2,1,0:T(8,128)(2,1)} %copy-done.9), calls=%async_computation.3 | async-start | bytes 1966080 | tf_op jit(solution)/shard_map/all_to_all | solution.py:231
  104.5 24.1 %collective-permute-start.3 = (bf16[16,3,40,240]{3,2,1,0:T(8,128)(2,1)S(1)}, bf16[16,3,40,240]{3,2,1,0:T(8,128)(2,1)S(1)}, u32[]{:S(2)}, u32[]{:S(2)}) collective-permute-start(bf16[16,3,40,240]{3,2,1,0:T(8,128)(2,1)S(1)} %dft.18), channel_id=1, source_target_pairs={{0,2},{1,3},{2,0},{3,1},{4,6},{5,7},{6,4},{7,5},{8,10},{9,11},{10,... | collective-permute-start | bytes 2764808 | tf_op jit(solution)/shard_map/ppermute | solution.py:227
  133.2 39.9 %all-to-all-start.4 = ((bf16[16,3,40,240]{3,2,1,0:T(8,128)(2,1)}), bf16[16,3,40,240]{3,2,1,0:T(8,128)(2,1)}, u32[]{:S(2)}, u32[]{:S(2)}) async-start(bf16[16,3,40,240]{3,2,1,0:T(8,128)(2,1)} %copy-done.10), calls=%async_computation.4 | async-start | bytes 1966080 | tf_op jit(solution)/shard_map/all_to_all | solution.py:231
  144.3 24.1 %collective-permute-start.4 = (bf16[16,3,40,240]{3,2,1,0:T(8,128)(2,1)S(1)}, bf16[16,3,40,240]{3,2,1,0:T(8,128)(2,1)S(1)}, u32[]{:S(2)}, u32[]{:S(2)}) collective-permute-start(bf16[16,3,40,240]{3,2,1,0:T(8,128)(2,1)S(1)} %dft.20), channel_id=1, source_target_pairs={{0,2},{1,3},{2,0},{3,1},{4,6},{5,7},{6,4},{7,5},{8,10},{9,11},{10,... | collective-permute-start | bytes 2764808 | tf_op jit(solution)/shard_map/ppermute | solution.py:227
  173.1 39.8 %all-to-all-start.5 = ((bf16[16,3,40,240]{3,2,1,0:T(8,128)(2,1)}), bf16[16,3,40,240]{3,2,1,0:T(8,128)(2,1)}, u32[]{:S(2)}, u32[]{:S(2)}) async-start(bf16[16,3,40,240]{3,2,1,0:T(8,128)(2,1)} %copy-done.11), calls=%async_computation.5 | async-start | bytes 1966080 | tf_op jit(solution)/shard_map/all_to_all | solution.py:231
  184.1 24.1 %collective-permute-start.5 = (bf16[16,3,40,240]{3,2,1,0:T(8,128)(2,1)S(1)}, bf16[16,3,40,240]{3,2,1,0:T(8,128)(2,1)S(1)}, u32[]{:S(2)}, u32[]{:S(2)}) collective-permute-start(bf16[16,3,40,240]{3,2,1,0:T(8,128)(2,1)S(1)} %dft.22), channel_id=1, source_target_pairs={{0,2},{1,3},{2,0},{3,1},{4,6},{5,7},{6,4},{7,5},{8,10},{9,11},{10,... | collective-permute-start | bytes 2764808 | tf_op jit(solution)/shard_map/ppermute | solution.py:227
  212.9 41.1 %all-to-all-start.6 = ((bf16[16,3,40,240]{3,2,1,0:T(8,128)(2,1)}), bf16[16,3,40,240]{3,2,1,0:T(8,128)(2,1)}, u32[]{:S(2)}, u32[]{:S(2)}) async-start(bf16[16,3,40,240]{3,2,1,0:T(8,128)(2,1)} %copy-done.7), calls=%async_computation.6 | async-start | bytes 1966080 | tf_op jit(solution)/shard_map/all_to_all | solution.py:231
  220.2 6.2 %copy-start.20 = (f32[3,3,12]{2,1,0:T(4,128)S(1)}, f32[3,3,12]{2,1,0:T(4,128)}, u32[]{:S(2)}) copy-start(f32[3,3,12]{2,1,0:T(4,128)} %param.11) | copy-start | bytes 1300
  220.2 6.8 %copy-start.21 = (f32[3,3,12]{2,1,0:T(4,128)S(1)}, f32[3,3,12]{2,1,0:T(4,128)}, u32[]{:S(2)}) copy-start(f32[3,3,12]{2,1,0:T(4,128)} %param.12) | copy-start | bytes 1300
  220.2 7.4 %copy-start.22 = (f32[3,3,12]{2,1,0:T(4,128)S(1)}, f32[3,3,12]{2,1,0:T(4,128)}, u32[]{:S(2)}) copy-start(f32[3,3,12]{2,1,0:T(4,128)} %param.13) | copy-start | bytes 1300
  220.2 8.0 %copy-start.25 = (s32[8]{0:T(128)S(1)}, s32[8]{0:T(128)}, u32[]{:S(2)}) copy-start(s32[8]{0:T(128)} %param.9) | copy-start | bytes 100
  224.8 24.3 %collective-permute-start = (bf16[16,3,40,240]{3,2,1,0:T(8,128)(2,1)}, bf16[16,3,40,240]{3,2,1,0:T(8,128)(2,1)}, u32[]{:S(2)}, u32[]{:S(2)}) collective-permute-start(bf16[16,3,40,240]{3,2,1,0:T(8,128)(2,1)} %dft.12), channel_id=1, source_target_pairs={{0,2},{1,3},{2,0},{3,1},{4,6},{5,7},{6,4},{7,5},{8,10},{9,11},{10,... | collective-permute-start | bytes 2764808 | tf_op jit(solution)/shard_map/ppermute | solution.py:227
  254.0 51.2 %all-to-all-start.1 = ((bf16[16,3,40,240]{3,2,1,0:T(8,128)(2,1)}), bf16[16,3,40,240]{3,2,1,0:T(8,128)(2,1)S(1)}, u32[]{:S(2)}, u32[]{:S(2)}) async-start(bf16[16,3,40,240]{3,2,1,0:T(8,128)(2,1)} %copy-done.8), calls=%async_computation.1 | async-start | bytes 1966080 | tf_op jit(solution)/shard_map/all_to_all | solution.py:231
  305.2 8.3 %copy-start.18 = (bf16[2,3,40,1280]{3,2,1,0:T(8,128)(2,1)S(1)}, bf16[2,3,40,1280]{3,2,1,0:T(8,128)(2,1)}, u32[]{:S(2)}) copy-start(bf16[2,3,40,1280]{3,2,1,0:T(8,128)(2,1)} %copy-done.17) | copy-start | bytes 1843204
  305.2 8.3 %copy-start.16 = (bf16[2,3,40,1280]{3,2,1,0:T(8,128)(2,1)S(1)}, bf16[2,3,40,1280]{3,2,1,0:T(8,128)(2,1)}, u32[]{:S(2)}) copy-start(bf16[2,3,40,1280]{3,2,1,0:T(8,128)(2,1)} %copy-done.15) | copy-start | bytes 1843204
  305.2 8.4 %copy-start.14 = (bf16[2,3,40,1280]{3,2,1,0:T(8,128)(2,1)S(1)}, bf16[2,3,40,1280]{3,2,1,0:T(8,128)(2,1)}, u32[]{:S(2)}) copy-start(bf16[2,3,40,1280]{3,2,1,0:T(8,128)(2,1)} %copy-done.13) | copy-start | bytes 1843204
  (15 other events, 18.1 us)

commit v2 on v1

--- a/solution.py
+++ b/solution.py
@@ -93,32 +93,29 @@
     )(*operands)
 
 
-def place_kernel(place_ref, in_ref, out_ref):
-    bands, _, count, rows, slots = in_ref.shape
-    for q in range(count):
-        total = jnp.dot(in_ref[0, 0, q], place_ref[0], preferred_element_type=jnp.float32)
-        for band in range(1, bands):
-            total += jnp.dot(in_ref[band, 0, q], place_ref[band], preferred_element_type=jnp.float32)
-        out_ref[0, q] = total.astype(jnp.bfloat16)
-
-
-def place_rows(place, arrived):
-    bands, pair, count, rows, slots = arrived.shape
+def place_kernel(place_ref, order_ref, in_ref, out_ref):
+    bands = in_ref.shape[0]
+    slots, width, lats = out_ref.shape
+    total = jnp.zeros((slots * width, lats), jnp.float32)
+    for band in range(bands):
+        ordered = jnp.dot(order_ref[...], in_ref[band], preferred_element_type=jnp.float32)
+        total += jnp.dot(ordered.astype(jnp.bfloat16), place_ref[band], preferred_element_type=jnp.float32)
+    out_ref[...] = total.astype(jnp.bfloat16).reshape(slots, width, lats)
+
+
+def place_rows(place, order, arrived, slots):
+    bands, rows, slot_rows = arrived.shape
     lats = place.shape[2]
-    flops = 2 * pair * count * rows * bands * slots * lats
+    flops = 2 * order.shape[0] * bands * slot_rows * lats
     return pl.pallas_call(
         place_kernel,
-        grid=(pair,),
-        in_specs=[
-            pl.BlockSpec(place.shape, lambda i: (0, 0, 0)),
-            pl.BlockSpec((bands, 1, count, rows, slots), lambda i: (0, i, 0, 0, 0)),
-        ],
-        out_specs=pl.BlockSpec((1, count, rows, lats), lambda i: (i, 0, 0, 0)),
-        out_shape=jax.ShapeDtypeStruct((pair, count, rows, lats), jnp.bfloat16),
-        compiler_params=params(),
-        cost_estimate=pl.CostEstimate(flops=flops, bytes_accessed=place.size * 2, transcendentals=0),
+        out_shape=jax.ShapeDtypeStruct((slots, order.shape[0] // slots, lats), jnp.bfloat16),
+        in_specs=[pl.BlockSpec(memory_space=pltpu.VMEM)] * 3,
+        out_specs=pl.BlockSpec(memory_space=pltpu.VMEM),
+        compiler_params=params(),
+        cost_estimate=pl.CostEstimate(flops=2 * flops, bytes_accessed=place.size * 2, transcendentals=0),
         name="place",
-    )(place, arrived)
+    )(place, order, arrived)
 
 
 def solve_kernel(lower_ref, inverse_ref, upper_ref, out_ref, *, fields, levels):
@@ -155,12 +152,13 @@
     return whole[:, :fields * levels]
 
 
-def legendre_kernel(owner_ref, mix_ref, panel_ref, legendre_ref, out_ref):
+def legendre_kernel(owner_ref, mix_ref, legendre_ref, *rest):
+    out_ref = rest[-1]
     slot = pl.program_id(0)
-    total = jnp.dot(panel_ref[0], legendre_ref[0], preferred_element_type=jnp.float32)
+    panel = jnp.concatenate([ref[0] for ref in rest[:-1]], axis=0)
+    total = jnp.dot(panel, legendre_ref[0], preferred_element_type=jnp.float32)
     high = total.astype(jnp.bfloat16)
     low = (total - high.astype(jnp.float32)).astype(jnp.bfloat16)
-    count = total.shape[0]
     mixed = jnp.dot(mix_ref[0], high, preferred_element_type=jnp.float32)
     mixed += jnp.dot(mix_ref[0], low, preferred_element_type=jnp.float32)
     mixed += jnp.dot(mix_ref[1], high, preferred_element_type=jnp.float32)
@@ -169,7 +167,8 @@
 
 
 def project(owners, mix, panels, legendre):
-    slots, rows, lats = panels.shape
+    slots, width, lats = panels[0].shape
+    rows = mix.shape[1]
     degrees = legendre.shape[2]
     return pl.pallas_call(
         legendre_kernel,
@@ -177,14 +176,13 @@
         in_specs=[
             pl.BlockSpec(memory_space=pltpu.SMEM),
             pl.BlockSpec(mix.shape, lambda i: (0, 0, 0)),
-            pl.BlockSpec((1, rows, lats), lambda i: (i, 0, 0)),
             pl.BlockSpec((1, lats, degrees), lambda i: (i, 0, 0)),
-        ],
+        ] + [pl.BlockSpec((1, width, lats), lambda i: (i, 0, 0))] * len(panels),
         out_specs=pl.BlockSpec((1, rows, degrees), lambda i: (i, 0, 0)),
         out_shape=jax.ShapeDtypeStruct((slots, rows, degrees), jnp.float32),
         compiler_params=params(),
         name="legendre",
-    )(owners, mix, panels, legendre)
+    )(owners, mix, legendre, *panels)
 
 
 def shards(bands, pairs, grid_fields, band_rows, wave_owner, lower_blocks, pivot_inverse, upper_blocks, legendre):
@@ -219,26 +217,46 @@
 
     dests = 2 * bands
     count = half // CHUNKS
-    across = [(2 * y + c, 2 * (1 - y) + c) for y in range(2) for c in range(2)]
+    across = [(2 * y + c, 2 * (1 - y) + c) for y in range(pairs) for c in range(2)]
     teams = [[aa * group + 2 * y + c for aa in range(bands) for c in range(2)] for y in range(pairs)]
-    sent = []
-    for chunk in range(CHUNKS):
-        part = dft(tables[0], grid, chunk * count, count, dests)
-        sent.append(lax.ppermute(part, "ba", across))
+    width = -(-4 * count // 16) * 16
+    order = np.zeros((per * width, 2 * count * rows), np.float32)
+    wide = np.full(CHUNKS * width, -1)
+    for member in range(2):
+        for q in range(count):
+            for part in range(2):
+                line = (part * 2 + member) * count + q
+                for i in range(per):
+                    order[i * width + line, (member * count + q) * rows + part * per + i] = 1
+                for chunk in range(CHUNKS):
+                    wide[chunk * width + line] = part * columns + member * half + chunk * count + q
+    order = jnp.asarray(order, jnp.bfloat16)
+
+    operator = vertical_operator(lower_blocks, pivot_inverse, upper_blocks)
+    mix = jnp.kron(jnp.eye(2, dtype=jnp.float32), operator)
+    mix = jnp.where(wide[None, :] >= 0, jnp.take(mix, np.maximum(wide, 0), axis=1), 0.0)
+    high = mix.astype(jnp.bfloat16)
+    low = (mix - high.astype(jnp.float32)).astype(jnp.bfloat16)
+    mix = jnp.stack([high, low])
+
+    parts = dft(tables[0], grid, 0, count, dests)
+    sent = [lax.ppermute(parts, "ba", across)]
     placed = []
     for chunk in range(CHUNKS):
-        full = dft(tables[1], grid, chunk * count, count, dests, sent[chunk])
+        came = sent[chunk]
+        if chunk + 1 < CHUNKS:
+            parts = dft(tables[0], grid, (chunk + 1) * count, count, dests)
+            came, parts = lax.optimization_barrier((came, parts))
+            sent.append(lax.ppermute(parts, "ba", across))
+        if chunk >= 2:
+            came, placed[chunk - 2] = lax.optimization_barrier((came, placed[chunk - 2]))
+        full = dft(tables[1], grid, chunk * count, count, dests, came)
         arrived = lax.all_to_all(full, ("aa", "ba"), split_axis=0, concat_axis=0, axis_index_groups=teams, tiled=True)
-        placed.append(place_rows(place, arrived.reshape(bands, 2, count, rows, slot_rows)))
-    panels = jnp.stack(placed, axis=1)[:, :, :, :2 * per].reshape(columns, 2, per, lats)
-    panels = jnp.transpose(panels, (2, 1, 0, 3)).reshape(per, 2 * columns, lats)
-
-    operator = vertical_operator(lower_blocks, pivot_inverse, upper_blocks)
-    mix = jnp.kron(jnp.eye(2, dtype=jnp.float32), operator)
-    high = mix.astype(jnp.bfloat16)
-    low = (mix - high.astype(jnp.float32)).astype(jnp.bfloat16)
+        arrived = arrived.reshape(bands, 2 * count * rows, slot_rows)
+        placed.append(place_rows(place, order, arrived, per))
+
     mine = lax.dynamic_slice_in_dim(wave_owner, (a * group + b) * per, per)
-    return project(mine, jnp.stack([high, low]), panels, legendre)
+    return project(mine, mix, placed, legendre)
 
 
 def solution(mesh):

time: 367 us -> 298 us (0.81)
  waiting for transfers between devices: 131 us -> 95.9 us
  local copies, waits for them, and re-layouts: 40.9 us -> 20.3 us
  Pallas kernels: 132 us -> 119 us
    ppermute x6, waiting for transfers between devices: 126 us -> 79 us  [the longest x5 67.5 us: shards(): sent.append(lax.ppermute(parts, 'ba', across))]
    pallas_call x6, Pallas kernels: 47.9 us -> 31.3 us  [place_rows(): pl.pallas_call(place_kernel, out_shape=jax.ShapeDtypeStruct((slots, order...]
    reshape x2 -> x0, local copies, waits for them, and re-layouts: 12.9 us -> none  [the longest x1 6.55 us: shards(): jnp.stack(placed, axis=1)[:, :, :, :2 * per].reshape(columns, 2, per, lats)]
    all_to_all x6, waiting for transfers between devices: 0.02 us -> 11.6 us  [shards(): lax.all_to_all(full, ('aa', 'ba'), split_axis=0, concat_axis=0, axis_inde...]
    transpose x1 -> x0, local copies, waits for them, and re-layouts: 5.38 us -> none  [shards(): panels = jnp.transpose(panels, (2, 1, 0, 3)).reshape(per, 2 * columns, lats)]
    pallas_call x12, Pallas kernels: 45.4 us -> 49.5 us  [dft(): pl.pallas_call(dft_kernel, grid=(count,), in_specs=in_specs, out_specs=ou...]
    unnamed x57 -> x66, local copies, waits for them, and re-layouts: 18.2 us -> 16.5 us
  transfers between devices with their start and end apart: 13 -> 13, of which waited for: 7 -> 8; matrix products, arithmetic and copies ran while one was open for 2% -> 3% of each run, Pallas kernels for 24% -> 26%
where the time goes in v2:
time: 298 us; the launch traced here: 295 us
  Pallas kernels  119 us (40%)
  waiting for transfers between devices  95.9 us (32%)
  starting transfers between devices  54.4 us (18%)
  local copies, waits for them, and re-layouts  20.3 us (7%)
  other arithmetic  4.36 us (1%)
    ppermute x5, waiting for transfers between devices, shards(): sent.append(lax.ppermute(parts, 'ba', across))  67.5 us
    pallas_call x12, Pallas kernels, dft(): pl.pallas_call(dft_kernel, grid=(count,), in_specs=in_specs, out_specs=ou...  49.5 us
    all_to_all x6, starting transfers between devices, shards(): lax.all_to_all(full, ('aa', 'ba'), split_axis=0, concat_axis=0, axis_inde...  34.9 us
    pallas_call x6, Pallas kernels, place_rows(): pl.pallas_call(place_kernel, out_shape=jax.ShapeDtypeStruct((slots, order...  31.3 us
    pallas_call x1, Pallas kernels, project(): pl.pallas_call(legendre_kernel, grid=(slots,), in_specs=[pl.BlockSpec(mem...  28.1 us
    unnamed x66, local copies, waits for them, and re-layouts  16.5 us
    all_to_all x6, waiting for transfers between devices, shards(): lax.all_to_all(full, ('aa', 'ba'), split_axis=0, concat_axis=0, axis_inde...  11.6 us
    ppermute x1, waiting for transfers between devices, shards(): sent = [lax.ppermute(parts, 'ba', across)]  11.5 us
  transfers between devices with their start and end apart: 13, of which 8 were waited for; matrix products, arithmetic and copies ran while one was open for 3% of the time, Pallas kernels for 26%

profile of v2, /device:TPU:0, one launch (start us, length us, event | category | flops | bytes accessed | tf_op | source)
XLA Modules:
  0.0 294.7 jit_solution(8574854002700553591)
XLA Ops:
  0.0 8.7 %all-to-all-start = ((bf16[2,18,240,768]{3,2,1,0:T(8,128)(2,1)}), bf16[2,18,240,768]{3,2,1,0:T(8,128)(2,1)}, u32[]{:S(2)}, u32[]{:S(2)}) async-start(bf16[2,18,240,768]{3,2,1,0:T(8,128)(2,1)} %bitcast.34), calls=%async_computation | async-start | bytes 26542080 | tf_op jit(solution)/shard_map/all_to_all | solution.py:199
  14.4 5.4 %all-to-all-done.grid_ref = bf16[2,18,240,768]{3,2,1,0:T(8,128)(2,1)} async-done(((bf16[2,18,240,768]{3,2,1,0:T(8,128)(2,1)}), bf16[2,18,240,768]{3,2,1,0:T(8,128)(2,1)}, u32[]{:S(2)}, u32[]{:S(2)}) %all-to-all-start) | async-done | bytes 13271072 | tf_op jit(solution)/shard_map/all_to_all | solution.py:199
  37.0 11.5 %collective-permute-done.rest_0_ = bf16[16,3,40,240]{3,2,1,0:T(8,128)(2,1)S(1)} collective-permute-done((bf16[16,3,40,240]{3,2,1,0:T(8,128)(2,1)S(1)}, bf16[16,3,40,240]{3,2,1,0:T(8,128)(2,1)S(1)}, u32[]{:S(2)}, u32[]{:S(2)}) %collective-permute-start) | collective-permute-done | bytes 921632 | tf_op jit(solution)/shard_map/ppermute | solution.py:243
  53.0 6.1 %all-to-all-start.1 = ((bf16[16,3,40,240]{3,2,1,0:T(8,128)(2,1)}), bf16[16,3,40,240]{3,2,1,0:T(8,128)(2,1)S(1)}, u32[]{:S(2)}, u32[]{:S(2)}) async-start(bf16[16,3,40,240]{3,2,1,0:T(8,128)(2,1)} %dft.16), calls=%async_computation.1 | async-start | bytes 1966080 | tf_op jit(solution)/shard_map/all_to_all | solution.py:254
  66.9 16.5 %collective-permute-done.1.rest_0_ = bf16[16,3,40,240]{3,2,1,0:T(8,128)(2,1)S(1)} collective-permute-done((bf16[16,3,40,240]{3,2,1,0:T(8,128)(2,1)}, bf16[16,3,40,240]{3,2,1,0:T(8,128)(2,1)S(1)}, u32[]{:S(2)}, u32[]{:S(2)}) %collective-permute-start.1) | collective-permute-done | bytes 921632 | tf_op jit(solution)/shard_map/ppermute | solution.py:250
  83.4 4.5 %dft.18 = bf16[16,3,40,240]{3,2,1,0:T(8,128)(2,1)} custom-call(bf16[640,1536]{1,0:T(8,128)(2,1)S(1)} %table.3.table_ref, bf16[2,18,240,768]{3,2,1,0:T(8,128)(2,1)} %all-to-all-done.grid_ref, bf16[16,3,40,240]{3,2,1,0:T(8,128)(2,1)S(1)} %collective-permute-done.1.rest_0_), custom_call_target="tpu_custom_call" | custom-call | flops 1415577600 | bytes 6286080 | tf_op jit(solution)/shard_map/dft/pallas_call | solution.py:84
  88.9 5.7 %all-to-all-start.2 = ((bf16[16,3,40,240]{3,2,1,0:T(8,128)(2,1)}), bf16[16,3,40,240]{3,2,1,0:T(8,128)(2,1)S(1)}, u32[]{:S(2)}, u32[]{:S(2)}) async-start(bf16[16,3,40,240]{3,2,1,0:T(8,128)(2,1)} %dft.18), calls=%async_computation.2 | async-start | bytes 1966080 | tf_op jit(solution)/shard_map/all_to_all | solution.py:254
  105.0 5.0 %place.6.rest_0_ = bf16[20,16,1280]{2,1,0:T(8,128)(2,1)S(1)} custom-call(bf16[8,240,1280]{2,1,0:T(8,128)(2,1)} %fusion.place_ref, bf16[320,240]{1,0:T(8,128)(2,1)S(1)} %copy-done.24, bf16[8,240,240]{2,1,0:T(8,128)(2,1)S(1)} %bitcast.32), custom_call_target="tpu_custom_call" | custom-call | flops 3145728000 | bytes 4915200 | tf_op jit(solution)/shard_map/place/pallas_call | solution.py:110
  110.9 13.5 %collective-permute-done.2.rest_0_ = bf16[16,3,40,240]{3,2,1,0:T(8,128)(2,1)S(1)} collective-permute-done((bf16[16,3,40,240]{3,2,1,0:T(8,128)(2,1)S(1)}, bf16[16,3,40,240]{3,2,1,0:T(8,128)(2,1)S(1)}, u32[]{:S(2)}, u32[]{:S(2)}) %collective-permute-start.2) | collective-permute-done | bytes 921632 | tf_op jit(solution)/shard_map/ppermute | solution.py:250
  129.0 5.8 %all-to-all-start.3 = ((bf16[16,3,40,240]{3,2,1,0:T(8,128)(2,1)}), bf16[16,3,40,240]{3,2,1,0:T(8,128)(2,1)}, u32[]{:S(2)}, u32[]{:S(2)}) async-start(bf16[16,3,40,240]{3,2,1,0:T(8,128)(2,1)} %dft.20), calls=%async_computation.3 | async-start | bytes 1966080 | tf_op jit(solution)/shard_map/all_to_all | solution.py:254
  141.6 5.4 %place.7.rest_1_ = bf16[20,16,1280]{2,1,0:T(8,128)(2,1)S(1)} custom-call(bf16[8,240,1280]{2,1,0:T(8,128)(2,1)} %fusion.place_ref, bf16[320,240]{1,0:T(8,128)(2,1)S(1)} %copy-done.24, bf16[8,240,240]{2,1,0:T(8,128)(2,1)S(1)} %bitcast.31), custom_call_target="tpu_custom_call" | custom-call | flops 3145728000 | bytes 4915200 | tf_op jit(solution)/shard_map/place/pallas_call | solution.py:110
  147.9 11.1 %collective-permute-done.3.rest_0_ = bf16[16,3,40,240]{3,2,1,0:T(8,128)(2,1)S(1)} collective-permute-done((bf16[16,3,40,240]{3,2,1,0:T(8,128)(2,1)}, bf16[16,3,40,240]{3,2,1,0:T(8,128)(2,1)S(1)}, u32[]{:S(2)}, u32[]{:S(2)}) %collective-permute-start.3) | collective-permute-done | bytes 921632 | tf_op jit(solution)/shard_map/ppermute | solution.py:250
  163.5 5.7 %all-to-all-start.4 = ((bf16[16,3,40,240]{3,2,1,0:T(8,128)(2,1)}), bf16[16,3,40,240]{3,2,1,0:T(8,128)(2,1)S(1)}, u32[]{:S(2)}, u32[]{:S(2)}) async-start(bf16[16,3,40,240]{3,2,1,0:T(8,128)(2,1)} %dft.21), calls=%async_computation.4 | async-start | bytes 1966080 | tf_op jit(solution)/shard_map/all_to_all | solution.py:254
  176.1 5.7 %place.8.rest_2_ = bf16[20,16,1280]{2,1,0:T(8,128)(2,1)S(1)} custom-call(bf16[8,240,1280]{2,1,0:T(8,128)(2,1)} %fusion.place_ref, bf16[320,240]{1,0:T(8,128)(2,1)S(1)} %copy-done.24, bf16[8,240,240]{2,1,0:T(8,128)(2,1)} %bitcast.10.in_ref), custom_call_target="tpu_custom_call" | custom-call | flops 3145728000 | bytes 4915200 | tf_op jit(solution)/shard_map/place/pallas_call | solution.py:110
  182.7 10.8 %collective-permute-done.4.rest_0_ = bf16[16,3,40,240]{3,2,1,0:T(8,128)(2,1)S(1)} collective-permute-done((bf16[16,3,40,240]{3,2,1,0:T(8,128)(2,1)}, bf16[16,3,40,240]{3,2,1,0:T(8,128)(2,1)S(1)}, u32[]{:S(2)}, u32[]{:S(2)}) %collective-permute-start.4) | collective-permute-done | bytes 921632 | tf_op jit(solution)/shard_map/ppermute | solution.py:250
  193.6 4.6 %dft.22 = bf16[16,3,40,240]{3,2,1,0:T(8,128)(2,1)} custom-call(bf16[640,1536]{1,0:T(8,128)(2,1)S(1)} %table.3.table_ref, bf16[2,18,240,768]{3,2,1,0:T(8,128)(2,1)} %all-to-all-done.grid_ref, bf16[16,3,40,240]{3,2,1,0:T(8,128)(2,1)S(1)} %collective-permute-done.4.rest_0_), custom_call_target="tpu_custom_call" | custom-call | flops 1415577600 | bytes 6286080 | tf_op jit(solution)/shard_map/dft/pallas_call | solution.py:84
  199.1 5.7 %all-to-all-start.5 = ((bf16[16,3,40,240]{3,2,1,0:T(8,128)(2,1)}), bf16[16,3,40,240]{3,2,1,0:T(8,128)(2,1)S(1)}, u32[]{:S(2)}, u32[]{:S(2)}) async-start(bf16[16,3,40,240]{3,2,1,0:T(8,128)(2,1)} %dft.22), calls=%async_computation.5 | async-start | bytes 1966080 | tf_op jit(solution)/shard_map/all_to_all | solution.py:254
  207.6 5.0 %place.9.rest_3_ = bf16[20,16,1280]{2,1,0:T(8,128)(2,1)S(1)} custom-call(bf16[8,240,1280]{2,1,0:T(8,128)(2,1)} %fusion.place_ref, bf16[320,240]{1,0:T(8,128)(2,1)S(1)} %copy-done.24, bf16[8,240,240]{2,1,0:T(8,128)(2,1)S(1)} %bitcast.33), custom_call_target="tpu_custom_call" | custom-call | flops 3145728000 | bytes 4915200 | tf_op jit(solution)/shard_map/place/pallas_call | solution.py:110
  213.6 15.5 %collective-permute-done.5.rest_0_ = bf16[16,3,40,240]{3,2,1,0:T(8,128)(2,1)S(1)} collective-permute-done((bf16[16,3,40,240]{3,2,1,0:T(8,128)(2,1)}, bf16[16,3,40,240]{3,2,1,0:T(8,128)(2,1)S(1)}, u32[]{:S(2)}, u32[]{:S(2)}) %collective-permute-start.5) | collective-permute-done | bytes 921632 | tf_op jit(solution)/shard_map/ppermute | solution.py:250
  233.6 5.8 %all-to-all-start.6 = ((bf16[16,3,40,240]{3,2,1,0:T(8,128)(2,1)}), bf16[16,3,40,240]{3,2,1,0:T(8,128)(2,1)S(1)}, u32[]{:S(2)}, u32[]{:S(2)}) async-start(bf16[16,3,40,240]{3,2,1,0:T(8,128)(2,1)} %dft.23), calls=%async_computation.6 | async-start | bytes 1966080 | tf_op jit(solution)/shard_map/all_to_all | solution.py:254
  244.7 5.0 %place.10.rest_4_ = bf16[20,16,1280]{2,1,0:T(8,128)(2,1)S(1)} custom-call(bf16[8,240,1280]{2,1,0:T(8,128)(2,1)} %fusion.place_ref, bf16[320,240]{1,0:T(8,128)(2,1)S(1)} %copy-done.24, bf16[8,240,240]{2,1,0:T(8,128)(2,1)S(1)} %bitcast.29), custom_call_target="tpu_custom_call" | custom-call | flops 3145728000 | bytes 4915200 | tf_op jit(solution)/shard_map/place/pallas_call | solution.py:110
  249.7 11.6 %all-to-all-done.6 = bf16[16,3,40,240]{3,2,1,0:T(8,128)(2,1)S(1)} async-done(((bf16[16,3,40,240]{3,2,1,0:T(8,128)(2,1)}), bf16[16,3,40,240]{3,2,1,0:T(8,128)(2,1)S(1)}, u32[]{:S(2)}, u32[]{:S(2)}) %all-to-all-start.6) | async-done | bytes 921632 | tf_op jit(solution)/shard_map/all_to_all | solution.py:254
  261.3 5.2 %place.11.rest_5_ = bf16[20,16,1280]{2,1,0:T(8,128)(2,1)S(1)} custom-call(bf16[8,240,1280]{2,1,0:T(8,128)(2,1)} %fusion.place_ref, bf16[320,240]{1,0:T(8,128)(2,1)S(1)} %copy-done.24, bf16[8,240,240]{2,1,0:T(8,128)(2,1)S(1)} %bitcast.30), custom_call_target="tpu_custom_call" | custom-call | flops 3145728000 | bytes 4915200 | tf_op jit(solution)/shard_map/place/pallas_call | solution.py:110
  266.5 28.1 %legendre.1 = f32[20,72,896]{2,1,0:T(8,128)} custom-call(s32[20]{0:T(128)S(1)} %dynamic_slice.10.owner_ref, bf16[2,72,96]{2,1,0:T(8,128)(2,1)S(1)} %pad_maximum_fusion.mix_ref, bf16[20,1280,896]{2,1,0:T(8,128)(2,1)} %legendre_ref.1, bf16[20,16,1280]{2,1,0:T(8,128)(2,1)S(1)} %copy-done.17, bf16[20,16,1280]{2,1,0:T(8,128)(2,1)S(1)} %copy-done.19, ...), custom_call_target="tpu_custom_call" | custom-call | tf_op jit(solution)/shard_map/legendre/pallas_call | solution.py:173
  (115 shorter events, 86.0 us)
Async XLA Ops:
  0.0 8.8 %copy-start.29 = (s32[640]{0:T(1024)S(1)}, s32[640]{0:T(1024)}, u32[]{:S(2)}) copy-start(s32[640]{0:T(1024)} %param.13) | copy-start | bytes 7684
  0.0 9.2 %copy-start.28 = (s32[640]{0:T(1024)S(1)}, s32[640]{0:T(1024)}, u32[]{:S(2)}) copy-start(s32[640]{0:T(1024)} %constant.109) | copy-start | bytes 7684
  0.0 19.7 %all-to-all-start = ((bf16[2,18,240,768]{3,2,1,0:T(8,128)(2,1)}), bf16[2,18,240,768]{3,2,1,0:T(8,128)(2,1)}, u32[]{:S(2)}, u32[]{:S(2)}) async-start(bf16[2,18,240,768]{3,2,1,0:T(8,128)(2,1)} %bitcast.34), calls=%async_computation | async-start | bytes 26542080 | tf_op jit(solution)/shard_map/all_to_all | solution.py:199
  14.4 9.1 %copy-start = (bf16[640,1536]{1,0:T(8,128)(2,1)}, bf16[640,1536]{1,0:T(8,128)(2,1)S(1)}, u32[]{:S(2)}) copy-start(bf16[640,1536]{1,0:T(8,128)(2,1)S(1)} %table.2.table_ref) | copy-start | bytes 5898244
  23.4 25.0 %collective-permute-start = (bf16[16,3,40,240]{3,2,1,0:T(8,128)(2,1)S(1)}, bf16[16,3,40,240]{3,2,1,0:T(8,128)(2,1)S(1)}, u32[]{:S(2)}, u32[]{:S(2)}) collective-permute-start(bf16[16,3,40,240]{3,2,1,0:T(8,128)(2,1)S(1)} %dft.12), channel_id=1, source_target_pairs={{0,2},{1,3},{2,0},{3,1},{4,6},{5,7},{6,4},{7,5},{8,10},{9,11},{10,... | collective-permute-start | bytes 2764808 | tf_op jit(solution)/shard_map/ppermute | solution.py:243
  53.0 35.0 %all-to-all-start.1 = ((bf16[16,3,40,240]{3,2,1,0:T(8,128)(2,1)}), bf16[16,3,40,240]{3,2,1,0:T(8,128)(2,1)S(1)}, u32[]{:S(2)}, u32[]{:S(2)}) async-start(bf16[16,3,40,240]{3,2,1,0:T(8,128)(2,1)} %dft.16), calls=%async_computation.1 | async-start | bytes 1966080 | tf_op jit(solution)/shard_map/all_to_all | solution.py:254
  59.1 24.3 %collective-permute-start.1 = (bf16[16,3,40,240]{3,2,1,0:T(8,128)(2,1)}, bf16[16,3,40,240]{3,2,1,0:T(8,128)(2,1)S(1)}, u32[]{:S(2)}, u32[]{:S(2)}) collective-permute-start(bf16[16,3,40,240]{3,2,1,0:T(8,128)(2,1)} %copy-done.15), channel_id=1, source_target_pairs={{0,2},{1,3},{2,0},{3,1},{4,6},{5,7},{6,4},{7,5},{8,10},{9,11},{10,... | collective-permute-start | bytes 2764808 | tf_op jit(solution)/shard_map/ppermute | solution.py:250
  66.9 27.8 %copy-start.31 = (s32[8]{0:T(128)S(1)}, s32[8]{0:T(128)}, u32[]{:S(2)}) copy-start(s32[8]{0:T(128)} %param.12) | copy-start | bytes 100
  88.9 40.1 %all-to-all-start.2 = ((bf16[16,3,40,240]{3,2,1,0:T(8,128)(2,1)}), bf16[16,3,40,240]{3,2,1,0:T(8,128)(2,1)S(1)}, u32[]{:S(2)}, u32[]{:S(2)}) async-start(bf16[16,3,40,240]{3,2,1,0:T(8,128)(2,1)} %dft.18), calls=%async_computation.2 | async-start | bytes 1966080 | tf_op jit(solution)/shard_map/all_to_all | solution.py:254
  96.4 8.6 %copy-start.24 = (bf16[320,240]{1,0:T(8,128)(2,1)S(1)}, bf16[320,240]{1,0:T(8,128)(2,1)}, u32[]{:S(2)}) copy-start(bf16[320,240]{1,0:T(8,128)(2,1)} %constant.97.clone.order_ref) | copy-start | bytes 460804
  100.3 9.7 %copy-start.8 = (bf16[16,3,40,240]{3,2,1,0:T(8,128)(2,1)}, bf16[16,3,40,240]{3,2,1,0:T(8,128)(2,1)S(1)}, u32[]{:S(2)}) copy-start(bf16[16,3,40,240]{3,2,1,0:T(8,128)(2,1)S(1)} %dft.15) | copy-start | bytes 2764804
  100.4 24.1 %collective-permute-start.2 = (bf16[16,3,40,240]{3,2,1,0:T(8,128)(2,1)S(1)}, bf16[16,3,40,240]{3,2,1,0:T(8,128)(2,1)S(1)}, u32[]{:S(2)}, u32[]{:S(2)}) collective-permute-start(bf16[16,3,40,240]{3,2,1,0:T(8,128)(2,1)S(1)} %copy-done.12), channel_id=1, source_target_pairs={{0,2},{1,3},{2,0},{3,1},{4,6},{5,7},{6,4},{7,5},{8,10},{9,11},{10,... | collective-permute-start | bytes 2764808 | tf_op jit(solution)/shard_map/ppermute | solution.py:250
  129.0 34.5 %all-to-all-start.3 = ((bf16[16,3,40,240]{3,2,1,0:T(8,128)(2,1)}), bf16[16,3,40,240]{3,2,1,0:T(8,128)(2,1)}, u32[]{:S(2)}, u32[]{:S(2)}) async-start(bf16[16,3,40,240]{3,2,1,0:T(8,128)(2,1)} %dft.20), calls=%async_computation.3 | async-start | bytes 1966080 | tf_op jit(solution)/shard_map/all_to_all | solution.py:254
  134.8 24.2 %collective-permute-start.3 = (bf16[16,3,40,240]{3,2,1,0:T(8,128)(2,1)}, bf16[16,3,40,240]{3,2,1,0:T(8,128)(2,1)S(1)}, u32[]{:S(2)}, u32[]{:S(2)}) collective-permute-start(bf16[16,3,40,240]{3,2,1,0:T(8,128)(2,1)} %copy-done.8), channel_id=1, source_target_pairs={{0,2},{1,3},{2,0},{3,1},{4,6},{5,7},{6,4},{7,5},{8,10},{9,11},{10,... | collective-permute-start | bytes 2764808 | tf_op jit(solution)/shard_map/ppermute | solution.py:250
  163.5 34.6 %all-to-all-start.4 = ((bf16[16,3,40,240]{3,2,1,0:T(8,128)(2,1)}), bf16[16,3,40,240]{3,2,1,0:T(8,128)(2,1)S(1)}, u32[]{:S(2)}, u32[]{:S(2)}) async-start(bf16[16,3,40,240]{3,2,1,0:T(8,128)(2,1)} %dft.21), calls=%async_computation.4 | async-start | bytes 1966080 | tf_op jit(solution)/shard_map/all_to_all | solution.py:254
  169.3 24.3 %collective-permute-start.4 = (bf16[16,3,40,240]{3,2,1,0:T(8,128)(2,1)}, bf16[16,3,40,240]{3,2,1,0:T(8,128)(2,1)S(1)}, u32[]{:S(2)}, u32[]{:S(2)}) collective-permute-start(bf16[16,3,40,240]{3,2,1,0:T(8,128)(2,1)} %copy-done.13), channel_id=1, source_target_pairs={{0,2},{1,3},{2,0},{3,1},{4,6},{5,7},{6,4},{7,5},{8,10},{9,11},{10,... | collective-permute-start | bytes 2764808 | tf_op jit(solution)/shard_map/ppermute | solution.py:250
  199.1 34.6 %all-to-all-start.5 = ((bf16[16,3,40,240]{3,2,1,0:T(8,128)(2,1)}), bf16[16,3,40,240]{3,2,1,0:T(8,128)(2,1)S(1)}, u32[]{:S(2)}, u32[]{:S(2)}) async-start(bf16[16,3,40,240]{3,2,1,0:T(8,128)(2,1)} %dft.22), calls=%async_computation.5 | async-start | bytes 1966080 | tf_op jit(solution)/shard_map/all_to_all | solution.py:254
  204.8 24.3 %collective-permute-start.5 = (bf16[16,3,40,240]{3,2,1,0:T(8,128)(2,1)}, bf16[16,3,40,240]{3,2,1,0:T(8,128)(2,1)S(1)}, u32[]{:S(2)}, u32[]{:S(2)}) collective-permute-start(bf16[16,3,40,240]{3,2,1,0:T(8,128)(2,1)} %copy-done.14), channel_id=1, source_target_pairs={{0,2},{1,3},{2,0},{3,1},{4,6},{5,7},{6,4},{7,5},{8,10},{9,11},{10,... | collective-permute-start | bytes 2764808 | tf_op jit(solution)/shard_map/ppermute | solution.py:250
  213.6 25.9 %copy-start.25 = (f32[3,3,12]{2,1,0:T(4,128)S(1)}, f32[3,3,12]{2,1,0:T(4,128)}, u32[]{:S(2)}) copy-start(f32[3,3,12]{2,1,0:T(4,128)} %param.14) | copy-start | bytes 1300
  213.6 26.5 %copy-start.26 = (f32[3,3,12]{2,1,0:T(4,128)S(1)}, f32[3,3,12]{2,1,0:T(4,128)}, u32[]{:S(2)}) copy-start(f32[3,3,12]{2,1,0:T(4,128)} %param.15) | copy-start | bytes 1300
  213.6 27.2 %copy-start.27 = (f32[3,3,12]{2,1,0:T(4,128)S(1)}, f32[3,3,12]{2,1,0:T(4,128)}, u32[]{:S(2)}) copy-start(f32[3,3,12]{2,1,0:T(4,128)} %param.16) | copy-start | bytes 1300
  213.6 30.3 %copy-start.32 = (s32[96]{0:T(128)S(1)}, s32[96]{0:T(128)}, u32[]{:S(2)}) copy-start(s32[96]{0:T(128)} %constant.111) | copy-start | bytes 1156
  213.6 31.0 %copy-start.30 = (pred[96]{0:T(512)(128)(4,1)S(1)}, pred[96]{0:T(512)(128)(4,1)}, u32[]{:S(2)}) copy-start(pred[96]{0:T(512)(128)(4,1)} %constant.101) | copy-start | bytes 292
  233.6 27.6 %all-to-all-start.6 = ((bf16[16,3,40,240]{3,2,1,0:T(8,128)(2,1)}), bf16[16,3,40,240]{3,2,1,0:T(8,128)(2,1)S(1)}, u32[]{:S(2)}, u32[]{:S(2)}) async-start(bf16[16,3,40,240]{3,2,1,0:T(8,128)(2,1)} %dft.23), calls=%async_computation.6 | async-start | bytes 1966080 | tf_op jit(solution)/shard_map/all_to_all | solution.py:254
  (22 other events, 60.9 us)

commit v3 on v2

--- a/solution.py
+++ b/solution.py
@@ -156,26 +156,27 @@
     out_ref = rest[-1]
     slot = pl.program_id(0)
     panel = jnp.concatenate([ref[0] for ref in rest[:-1]], axis=0)
-    total = jnp.dot(panel, legendre_ref[0], preferred_element_type=jnp.float32)
+    total = jnp.dot(mix_ref[...], jnp.concatenate([panel, panel], axis=0), preferred_element_type=jnp.float32)
     high = total.astype(jnp.bfloat16)
     low = (total - high.astype(jnp.float32)).astype(jnp.bfloat16)
-    mixed = jnp.dot(mix_ref[0], high, preferred_element_type=jnp.float32)
-    mixed += jnp.dot(mix_ref[0], low, preferred_element_type=jnp.float32)
-    mixed += jnp.dot(mix_ref[1], high, preferred_element_type=jnp.float32)
+    both = jnp.concatenate([high, low], axis=0)
+    both = jnp.dot(both, legendre_ref[0], preferred_element_type=jnp.float32)
+    count = total.shape[0]
+    mixed = both[:count] + both[count:]
     degree = lax.broadcasted_iota(jnp.int32, mixed.shape, 1)
     out_ref[0] = jnp.where(degree + owner_ref[slot] <= NT, mixed, 0.0)
 
 
 def project(owners, mix, panels, legendre):
     slots, width, lats = panels[0].shape
-    rows = mix.shape[1]
+    rows = mix.shape[0]
     degrees = legendre.shape[2]
     return pl.pallas_call(
         legendre_kernel,
         grid=(slots,),
         in_specs=[
             pl.BlockSpec(memory_space=pltpu.SMEM),
-            pl.BlockSpec(mix.shape, lambda i: (0, 0, 0)),
+            pl.BlockSpec(mix.shape, lambda i: (0, 0)),
             pl.BlockSpec((1, lats, degrees), lambda i: (i, 0, 0)),
         ] + [pl.BlockSpec((1, width, lats), lambda i: (i, 0, 0))] * len(panels),
         out_specs=pl.BlockSpec((1, rows, degrees), lambda i: (i, 0, 0)),
@@ -237,7 +238,7 @@
     mix = jnp.where(wide[None, :] >= 0, jnp.take(mix, np.maximum(wide, 0), axis=1), 0.0)
     high = mix.astype(jnp.bfloat16)
     low = (mix - high.astype(jnp.float32)).astype(jnp.bfloat16)
-    mix = jnp.stack([high, low])
+    mix = jnp.concatenate([high, low], axis=1)
 
     parts = dft(tables[0], grid, 0, count, dests)
     sent = [lax.ppermute(parts, "ba", across)]

time: 298 us -> 297 us (level)
  no operation moved by 1% of the time
where the time goes in v3:
time: 297 us; the launch traced here: 294 us
  Pallas kernels  118 us (40%)
  waiting for transfers between devices  95.8 us (32%)
  starting transfers between devices  54.4 us (18%)
  local copies, waits for them, and re-layouts  20.3 us (7%)
  other arithmetic  4.43 us (1%)
    ppermute x5, waiting for transfers between devices, shards(): sent.append(lax.ppermute(parts, 'ba', across))  67.5 us
    pallas_call x12, Pallas kernels, dft(): pl.pallas_call(dft_kernel, grid=(count,), in_specs=in_specs, out_specs=ou...  49.5 us
    all_to_all x6, starting transfers between devices, shards(): lax.all_to_all(full, ('aa', 'ba'), split_axis=0, concat_axis=0, axis_inde...  34.9 us
    pallas_call x6, Pallas kernels, place_rows(): pl.pallas_call(place_kernel, out_shape=jax.ShapeDtypeStruct((slots, order...  31.3 us
    pallas_call x1, Pallas kernels, project(): pl.pallas_call(legendre_kernel, grid=(slots,), in_specs=[pl.BlockSpec(mem...  27.4 us
    unnamed x66, local copies, waits for them, and re-layouts  16.5 us
    all_to_all x6, waiting for transfers between devices, shards(): lax.all_to_all(full, ('aa', 'ba'), split_axis=0, concat_axis=0, axis_inde...  11.5 us
    ppermute x1, waiting for transfers between devices, shards(): sent = [lax.ppermute(parts, 'ba', across)]  11.5 us
  transfers between devices with their start and end apart: 13, of which 8 were waited for; matrix products, arithmetic and copies ran while one was open for 3% of the time, Pallas kernels for 26%

profile of v3, /device:TPU:0, one launch (start us, length us, event | category | flops | bytes accessed | tf_op | source)
XLA Modules:
  0.0 293.9 jit_solution(357956371472708190)
XLA Ops:
  0.0 8.7 %all-to-all-start = ((bf16[2,18,240,768]{3,2,1,0:T(8,128)(2,1)}), bf16[2,18,240,768]{3,2,1,0:T(8,128)(2,1)}, u32[]{:S(2)}, u32[]{:S(2)}) async-start(bf16[2,18,240,768]{3,2,1,0:T(8,128)(2,1)} %bitcast.31), calls=%async_computation | async-start | bytes 26542080 | tf_op jit(solution)/shard_map/all_to_all | solution.py:200
  14.4 5.4 %all-to-all-done.grid_ref = bf16[2,18,240,768]{3,2,1,0:T(8,128)(2,1)} async-done(((bf16[2,18,240,768]{3,2,1,0:T(8,128)(2,1)}), bf16[2,18,240,768]{3,2,1,0:T(8,128)(2,1)}, u32[]{:S(2)}, u32[]{:S(2)}) %all-to-all-start) | async-done | bytes 13271072 | tf_op jit(solution)/shard_map/all_to_all | solution.py:200
  37.0 11.5 %collective-permute-done.rest_0_ = bf16[16,3,40,240]{3,2,1,0:T(8,128)(2,1)S(1)} collective-permute-done((bf16[16,3,40,240]{3,2,1,0:T(8,128)(2,1)S(1)}, bf16[16,3,40,240]{3,2,1,0:T(8,128)(2,1)S(1)}, u32[]{:S(2)}, u32[]{:S(2)}) %collective-permute-start) | collective-permute-done | bytes 921632 | tf_op jit(solution)/shard_map/ppermute | solution.py:244
  53.0 6.1 %all-to-all-start.1 = ((bf16[16,3,40,240]{3,2,1,0:T(8,128)(2,1)}), bf16[16,3,40,240]{3,2,1,0:T(8,128)(2,1)S(1)}, u32[]{:S(2)}, u32[]{:S(2)}) async-start(bf16[16,3,40,240]{3,2,1,0:T(8,128)(2,1)} %dft.16), calls=%async_computation.1 | async-start | bytes 1966080 | tf_op jit(solution)/shard_map/all_to_all | solution.py:255
  66.9 16.5 %collective-permute-done.1.rest_0_ = bf16[16,3,40,240]{3,2,1,0:T(8,128)(2,1)S(1)} collective-permute-done((bf16[16,3,40,240]{3,2,1,0:T(8,128)(2,1)}, bf16[16,3,40,240]{3,2,1,0:T(8,128)(2,1)S(1)}, u32[]{:S(2)}, u32[]{:S(2)}) %collective-permute-start.1) | collective-permute-done | bytes 921632 | tf_op jit(solution)/shard_map/ppermute | solution.py:251
  83.4 4.5 %dft.18 = bf16[16,3,40,240]{3,2,1,0:T(8,128)(2,1)} custom-call(bf16[640,1536]{1,0:T(8,128)(2,1)S(1)} %table.3.table_ref, bf16[2,18,240,768]{3,2,1,0:T(8,128)(2,1)} %all-to-all-done.grid_ref, bf16[16,3,40,240]{3,2,1,0:T(8,128)(2,1)S(1)} %collective-permute-done.1.rest_0_), custom_call_target="tpu_custom_call" | custom-call | flops 1415577600 | bytes 6286080 | tf_op jit(solution)/shard_map/dft/pallas_call | solution.py:84
  88.9 5.7 %all-to-all-start.2 = ((bf16[16,3,40,240]{3,2,1,0:T(8,128)(2,1)}), bf16[16,3,40,240]{3,2,1,0:T(8,128)(2,1)S(1)}, u32[]{:S(2)}, u32[]{:S(2)}) async-start(bf16[16,3,40,240]{3,2,1,0:T(8,128)(2,1)} %dft.18), calls=%async_computation.2 | async-start | bytes 1966080 | tf_op jit(solution)/shard_map/all_to_all | solution.py:255
  105.0 5.0 %place.6.rest_0_ = bf16[20,16,1280]{2,1,0:T(8,128)(2,1)S(1)} custom-call(bf16[8,240,1280]{2,1,0:T(8,128)(2,1)} %fusion.place_ref, bf16[320,240]{1,0:T(8,128)(2,1)S(1)} %copy-done.24, bf16[8,240,240]{2,1,0:T(8,128)(2,1)S(1)} %bitcast.29), custom_call_target="tpu_custom_call" | custom-call | flops 3145728000 | bytes 4915200 | tf_op jit(solution)/shard_map/place/pallas_call | solution.py:110
  110.9 13.5 %collective-permute-done.2.rest_0_ = bf16[16,3,40,240]{3,2,1,0:T(8,128)(2,1)S(1)} collective-permute-done((bf16[16,3,40,240]{3,2,1,0:T(8,128)(2,1)S(1)}, bf16[16,3,40,240]{3,2,1,0:T(8,128)(2,1)S(1)}, u32[]{:S(2)}, u32[]{:S(2)}) %collective-permute-start.2) | collective-permute-done | bytes 921632 | tf_op jit(solution)/shard_map/ppermute | solution.py:251
  129.0 5.8 %all-to-all-start.3 = ((bf16[16,3,40,240]{3,2,1,0:T(8,128)(2,1)}), bf16[16,3,40,240]{3,2,1,0:T(8,128)(2,1)}, u32[]{:S(2)}, u32[]{:S(2)}) async-start(bf16[16,3,40,240]{3,2,1,0:T(8,128)(2,1)} %dft.20), calls=%async_computation.3 | async-start | bytes 1966080 | tf_op jit(solution)/shard_map/all_to_all | solution.py:255
  141.6 5.4 %place.7.rest_1_ = bf16[20,16,1280]{2,1,0:T(8,128)(2,1)S(1)} custom-call(bf16[8,240,1280]{2,1,0:T(8,128)(2,1)} %fusion.place_ref, bf16[320,240]{1,0:T(8,128)(2,1)S(1)} %copy-done.24, bf16[8,240,240]{2,1,0:T(8,128)(2,1)S(1)} %bitcast.28), custom_call_target="tpu_custom_call" | custom-call | flops 3145728000 | bytes 4915200 | tf_op jit(solution)/shard_map/place/pallas_call | solution.py:110
  147.9 11.1 %collective-permute-done.3.rest_0_ = bf16[16,3,40,240]{3,2,1,0:T(8,128)(2,1)S(1)} collective-permute-done((bf16[16,3,40,240]{3,2,1,0:T(8,128)(2,1)}, bf16[16,3,40,240]{3,2,1,0:T(8,128)(2,1)S(1)}, u32[]{:S(2)}, u32[]{:S(2)}) %collective-permute-start.3) | collective-permute-done | bytes 921632 | tf_op jit(solution)/shard_map/ppermute | solution.py:251
  163.5 5.7 %all-to-all-start.4 = ((bf16[16,3,40,240]{3,2,1,0:T(8,128)(2,1)}), bf16[16,3,40,240]{3,2,1,0:T(8,128)(2,1)S(1)}, u32[]{:S(2)}, u32[]{:S(2)}) async-start(bf16[16,3,40,240]{3,2,1,0:T(8,128)(2,1)} %dft.21), calls=%async_computation.4 | async-start | bytes 1966080 | tf_op jit(solution)/shard_map/all_to_all | solution.py:255
  176.1 5.7 %place.8.rest_2_ = bf16[20,16,1280]{2,1,0:T(8,128)(2,1)S(1)} custom-call(bf16[8,240,1280]{2,1,0:T(8,128)(2,1)} %fusion.place_ref, bf16[320,240]{1,0:T(8,128)(2,1)S(1)} %copy-done.24, bf16[8,240,240]{2,1,0:T(8,128)(2,1)} %bitcast.9.in_ref), custom_call_target="tpu_custom_call" | custom-call | flops 3145728000 | bytes 4915200 | tf_op jit(solution)/shard_map/place/pallas_call | solution.py:110
  182.7 10.8 %collective-permute-done.4.rest_0_ = bf16[16,3,40,240]{3,2,1,0:T(8,128)(2,1)S(1)} collective-permute-done((bf16[16,3,40,240]{3,2,1,0:T(8,128)(2,1)}, bf16[16,3,40,240]{3,2,1,0:T(8,128)(2,1)S(1)}, u32[]{:S(2)}, u32[]{:S(2)}) %collective-permute-start.4) | collective-permute-done | bytes 921632 | tf_op jit(solution)/shard_map/ppermute | solution.py:251
  193.6 4.6 %dft.22 = bf16[16,3,40,240]{3,2,1,0:T(8,128)(2,1)} custom-call(bf16[640,1536]{1,0:T(8,128)(2,1)S(1)} %table.3.table_ref, bf16[2,18,240,768]{3,2,1,0:T(8,128)(2,1)} %all-to-all-done.grid_ref, bf16[16,3,40,240]{3,2,1,0:T(8,128)(2,1)S(1)} %collective-permute-done.4.rest_0_), custom_call_target="tpu_custom_call" | custom-call | flops 1415577600 | bytes 6286080 | tf_op jit(solution)/shard_map/dft/pallas_call | solution.py:84
  199.1 5.7 %all-to-all-start.5 = ((bf16[16,3,40,240]{3,2,1,0:T(8,128)(2,1)}), bf16[16,3,40,240]{3,2,1,0:T(8,128)(2,1)S(1)}, u32[]{:S(2)}, u32[]{:S(2)}) async-start(bf16[16,3,40,240]{3,2,1,0:T(8,128)(2,1)} %dft.22), calls=%async_computation.5 | async-start | bytes 1966080 | tf_op jit(solution)/shard_map/all_to_all | solution.py:255
  207.6 5.0 %place.9.rest_3_ = bf16[20,16,1280]{2,1,0:T(8,128)(2,1)S(1)} custom-call(bf16[8,240,1280]{2,1,0:T(8,128)(2,1)} %fusion.place_ref, bf16[320,240]{1,0:T(8,128)(2,1)S(1)} %copy-done.24, bf16[8,240,240]{2,1,0:T(8,128)(2,1)S(1)} %bitcast.30), custom_call_target="tpu_custom_call" | custom-call | flops 3145728000 | bytes 4915200 | tf_op jit(solution)/shard_map/place/pallas_call | solution.py:110
  213.6 15.5 %collective-permute-done.5.rest_0_ = bf16[16,3,40,240]{3,2,1,0:T(8,128)(2,1)S(1)} collective-permute-done((bf16[16,3,40,240]{3,2,1,0:T(8,128)(2,1)}, bf16[16,3,40,240]{3,2,1,0:T(8,128)(2,1)S(1)}, u32[]{:S(2)}, u32[]{:S(2)}) %collective-permute-start.5) | collective-permute-done | bytes 921632 | tf_op jit(solution)/shard_map/ppermute | solution.py:251
  233.6 5.8 %all-to-all-start.6 = ((bf16[16,3,40,240]{3,2,1,0:T(8,128)(2,1)}), bf16[16,3,40,240]{3,2,1,0:T(8,128)(2,1)S(1)}, u32[]{:S(2)}, u32[]{:S(2)}) async-start(bf16[16,3,40,240]{3,2,1,0:T(8,128)(2,1)} %dft.23), calls=%async_computation.6 | async-start | bytes 1966080 | tf_op jit(solution)/shard_map/all_to_all | solution.py:255
  244.7 5.0 %place.10.rest_4_ = bf16[20,16,1280]{2,1,0:T(8,128)(2,1)S(1)} custom-call(bf16[8,240,1280]{2,1,0:T(8,128)(2,1)} %fusion.place_ref, bf16[320,240]{1,0:T(8,128)(2,1)S(1)} %copy-done.24, bf16[8,240,240]{2,1,0:T(8,128)(2,1)S(1)} %bitcast.26), custom_call_target="tpu_custom_call" | custom-call | flops 3145728000 | bytes 4915200 | tf_op jit(solution)/shard_map/place/pallas_call | solution.py:110
  249.8 11.5 %all-to-all-done.6 = bf16[16,3,40,240]{3,2,1,0:T(8,128)(2,1)S(1)} async-done(((bf16[16,3,40,240]{3,2,1,0:T(8,128)(2,1)}), bf16[16,3,40,240]{3,2,1,0:T(8,128)(2,1)S(1)}, u32[]{:S(2)}, u32[]{:S(2)}) %all-to-all-start.6) | async-done | bytes 921632 | tf_op jit(solution)/shard_map/all_to_all | solution.py:255
  261.3 5.2 %place.11.rest_5_ = bf16[20,16,1280]{2,1,0:T(8,128)(2,1)S(1)} custom-call(bf16[8,240,1280]{2,1,0:T(8,128)(2,1)} %fusion.place_ref, bf16[320,240]{1,0:T(8,128)(2,1)S(1)} %copy-done.24, bf16[8,240,240]{2,1,0:T(8,128)(2,1)S(1)} %bitcast.27), custom_call_target="tpu_custom_call" | custom-call | flops 3145728000 | bytes 4915200 | tf_op jit(solution)/shard_map/place/pallas_call | solution.py:110
  266.5 27.4 %legendre.1 = f32[20,72,896]{2,1,0:T(8,128)} custom-call(s32[20]{0:T(128)S(1)} %dynamic_slice.10.owner_ref, bf16[72,192]{1,0:T(8,128)(2,1)S(1)} %pad_maximum_fusion.mix_ref, bf16[20,1280,896]{2,1,0:T(8,128)(2,1)} %legendre_ref.1, bf16[20,16,1280]{2,1,0:T(8,128)(2,1)S(1)} %copy-done.17, bf16[20,16,1280]{2,1,0:T(8,128)(2,1)S(1)} %copy-done.19, ...), custom_call_target="tpu_custom_call" | custom-call | tf_op jit(solution)/shard_map/legendre/pallas_call | solution.py:174
  (115 shorter events, 86.1 us)
Async XLA Ops:
  0.0 8.8 %copy-start.29 = (s32[640]{0:T(1024)S(1)}, s32[640]{0:T(1024)}, u32[]{:S(2)}) copy-start(s32[640]{0:T(1024)} %param.13) | copy-start | bytes 7684
  0.0 9.2 %copy-start.28 = (s32[640]{0:T(1024)S(1)}, s32[640]{0:T(1024)}, u32[]{:S(2)}) copy-start(s32[640]{0:T(1024)} %constant.109) | copy-start | bytes 7684
  0.0 19.7 %all-to-all-start = ((bf16[2,18,240,768]{3,2,1,0:T(8,128)(2,1)}), bf16[2,18,240,768]{3,2,1,0:T(8,128)(2,1)}, u32[]{:S(2)}, u32[]{:S(2)}) async-start(bf16[2,18,240,768]{3,2,1,0:T(8,128)(2,1)} %bitcast.31), calls=%async_computation | async-start | bytes 26542080 | tf_op jit(solution)/shard_map/all_to_all | solution.py:200
  14.4 9.1 %copy-start = (bf16[640,1536]{1,0:T(8,128)(2,1)}, bf16[640,1536]{1,0:T(8,128)(2,1)S(1)}, u32[]{:S(2)}) copy-start(bf16[640,1536]{1,0:T(8,128)(2,1)S(1)} %table.2.table_ref) | copy-start | bytes 5898244
  23.4 25.0 %collective-permute-start = (bf16[16,3,40,240]{3,2,1,0:T(8,128)(2,1)S(1)}, bf16[16,3,40,240]{3,2,1,0:T(8,128)(2,1)S(1)}, u32[]{:S(2)}, u32[]{:S(2)}) collective-permute-start(bf16[16,3,40,240]{3,2,1,0:T(8,128)(2,1)S(1)} %dft.12), channel_id=1, source_target_pairs={{0,2},{1,3},{2,0},{3,1},{4,6},{5,7},{6,4},{7,5},{8,10},{9,11},{10,... | collective-permute-start | bytes 2764808 | tf_op jit(solution)/shard_map/ppermute | solution.py:244
  53.0 35.0 %all-to-all-start.1 = ((bf16[16,3,40,240]{3,2,1,0:T(8,128)(2,1)}), bf16[16,3,40,240]{3,2,1,0:T(8,128)(2,1)S(1)}, u32[]{:S(2)}, u32[]{:S(2)}) async-start(bf16[16,3,40,240]{3,2,1,0:T(8,128)(2,1)} %dft.16), calls=%async_computation.1 | async-start | bytes 1966080 | tf_op jit(solution)/shard_map/all_to_all | solution.py:255
  59.1 24.3 %collective-permute-start.1 = (bf16[16,3,40,240]{3,2,1,0:T(8,128)(2,1)}, bf16[16,3,40,240]{3,2,1,0:T(8,128)(2,1)S(1)}, u32[]{:S(2)}, u32[]{:S(2)}) collective-permute-start(bf16[16,3,40,240]{3,2,1,0:T(8,128)(2,1)} %copy-done.15), channel_id=1, source_target_pairs={{0,2},{1,3},{2,0},{3,1},{4,6},{5,7},{6,4},{7,5},{8,10},{9,11},{10,... | collective-permute-start | bytes 2764808 | tf_op jit(solution)/shard_map/ppermute | solution.py:251
  66.9 27.8 %copy-start.31 = (s32[8]{0:T(128)S(1)}, s32[8]{0:T(128)}, u32[]{:S(2)}) copy-start(s32[8]{0:T(128)} %param.12) | copy-start | bytes 100
  88.9 40.1 %all-to-all-start.2 = ((bf16[16,3,40,240]{3,2,1,0:T(8,128)(2,1)}), bf16[16,3,40,240]{3,2,1,0:T(8,128)(2,1)S(1)}, u32[]{:S(2)}, u32[]{:S(2)}) async-start(bf16[16,3,40,240]{3,2,1,0:T(8,128)(2,1)} %dft.18), calls=%async_computation.2 | async-start | bytes 1966080 | tf_op jit(solution)/shard_map/all_to_all | solution.py:255
  96.4 8.6 %copy-start.24 = (bf16[320,240]{1,0:T(8,128)(2,1)S(1)}, bf16[320,240]{1,0:T(8,128)(2,1)}, u32[]{:S(2)}) copy-start(bf16[320,240]{1,0:T(8,128)(2,1)} %constant.97.clone.order_ref) | copy-start | bytes 460804
  100.3 9.7 %copy-start.8 = (bf16[16,3,40,240]{3,2,1,0:T(8,128)(2,1)}, bf16[16,3,40,240]{3,2,1,0:T(8,128)(2,1)S(1)}, u32[]{:S(2)}) copy-start(bf16[16,3,40,240]{3,2,1,0:T(8,128)(2,1)S(1)} %dft.15) | copy-start | bytes 2764804
  100.4 24.1 %collective-permute-start.2 = (bf16[16,3,40,240]{3,2,1,0:T(8,128)(2,1)S(1)}, bf16[16,3,40,240]{3,2,1,0:T(8,128)(2,1)S(1)}, u32[]{:S(2)}, u32[]{:S(2)}) collective-permute-start(bf16[16,3,40,240]{3,2,1,0:T(8,128)(2,1)S(1)} %copy-done.12), channel_id=1, source_target_pairs={{0,2},{1,3},{2,0},{3,1},{4,6},{5,7},{6,4},{7,5},{8,10},{9,11},{10,... | collective-permute-start | bytes 2764808 | tf_op jit(solution)/shard_map/ppermute | solution.py:251
  129.0 34.5 %all-to-all-start.3 = ((bf16[16,3,40,240]{3,2,1,0:T(8,128)(2,1)}), bf16[16,3,40,240]{3,2,1,0:T(8,128)(2,1)}, u32[]{:S(2)}, u32[]{:S(2)}) async-start(bf16[16,3,40,240]{3,2,1,0:T(8,128)(2,1)} %dft.20), calls=%async_computation.3 | async-start | bytes 1966080 | tf_op jit(solution)/shard_map/all_to_all | solution.py:255
  134.8 24.2 %collective-permute-start.3 = (bf16[16,3,40,240]{3,2,1,0:T(8,128)(2,1)}, bf16[16,3,40,240]{3,2,1,0:T(8,128)(2,1)S(1)}, u32[]{:S(2)}, u32[]{:S(2)}) collective-permute-start(bf16[16,3,40,240]{3,2,1,0:T(8,128)(2,1)} %copy-done.8), channel_id=1, source_target_pairs={{0,2},{1,3},{2,0},{3,1},{4,6},{5,7},{6,4},{7,5},{8,10},{9,11},{10,... | collective-permute-start | bytes 2764808 | tf_op jit(solution)/shard_map/ppermute | solution.py:251
  163.5 34.6 %all-to-all-start.4 = ((bf16[16,3,40,240]{3,2,1,0:T(8,128)(2,1)}), bf16[16,3,40,240]{3,2,1,0:T(8,128)(2,1)S(1)}, u32[]{:S(2)}, u32[]{:S(2)}) async-start(bf16[16,3,40,240]{3,2,1,0:T(8,128)(2,1)} %dft.21), calls=%async_computation.4 | async-start | bytes 1966080 | tf_op jit(solution)/shard_map/all_to_all | solution.py:255
  169.3 24.3 %collective-permute-start.4 = (bf16[16,3,40,240]{3,2,1,0:T(8,128)(2,1)}, bf16[16,3,40,240]{3,2,1,0:T(8,128)(2,1)S(1)}, u32[]{:S(2)}, u32[]{:S(2)}) collective-permute-start(bf16[16,3,40,240]{3,2,1,0:T(8,128)(2,1)} %copy-done.13), channel_id=1, source_target_pairs={{0,2},{1,3},{2,0},{3,1},{4,6},{5,7},{6,4},{7,5},{8,10},{9,11},{10,... | collective-permute-start | bytes 2764808 | tf_op jit(solution)/shard_map/ppermute | solution.py:251
  199.1 34.6 %all-to-all-start.5 = ((bf16[16,3,40,240]{3,2,1,0:T(8,128)(2,1)}), bf16[16,3,40,240]{3,2,1,0:T(8,128)(2,1)S(1)}, u32[]{:S(2)}, u32[]{:S(2)}) async-start(bf16[16,3,40,240]{3,2,1,0:T(8,128)(2,1)} %dft.22), calls=%async_computation.5 | async-start | bytes 1966080 | tf_op jit(solution)/shard_map/all_to_all | solution.py:255
  204.8 24.3 %collective-permute-start.5 = (bf16[16,3,40,240]{3,2,1,0:T(8,128)(2,1)}, bf16[16,3,40,240]{3,2,1,0:T(8,128)(2,1)S(1)}, u32[]{:S(2)}, u32[]{:S(2)}) collective-permute-start(bf16[16,3,40,240]{3,2,1,0:T(8,128)(2,1)} %copy-done.14), channel_id=1, source_target_pairs={{0,2},{1,3},{2,0},{3,1},{4,6},{5,7},{6,4},{7,5},{8,10},{9,11},{10,... | collective-permute-start | bytes 2764808 | tf_op jit(solution)/shard_map/ppermute | solution.py:251
  213.6 25.9 %copy-start.25 = (f32[3,3,12]{2,1,0:T(4,128)S(1)}, f32[3,3,12]{2,1,0:T(4,128)}, u32[]{:S(2)}) copy-start(f32[3,3,12]{2,1,0:T(4,128)} %param.14) | copy-start | bytes 1300
  213.6 26.5 %copy-start.26 = (f32[3,3,12]{2,1,0:T(4,128)S(1)}, f32[3,3,12]{2,1,0:T(4,128)}, u32[]{:S(2)}) copy-start(f32[3,3,12]{2,1,0:T(4,128)} %param.15) | copy-start | bytes 1300
  213.6 27.2 %copy-start.27 = (f32[3,3,12]{2,1,0:T(4,128)S(1)}, f32[3,3,12]{2,1,0:T(4,128)}, u32[]{:S(2)}) copy-start(f32[3,3,12]{2,1,0:T(4,128)} %param.16) | copy-start | bytes 1300
  213.6 30.3 %copy-start.32 = (s32[96]{0:T(128)S(1)}, s32[96]{0:T(128)}, u32[]{:S(2)}) copy-start(s32[96]{0:T(128)} %constant.111) | copy-start | bytes 1156
  213.6 31.0 %copy-start.30 = (pred[96]{0:T(512)(128)(4,1)S(1)}, pred[96]{0:T(512)(128)(4,1)}, u32[]{:S(2)}) copy-start(pred[96]{0:T(512)(128)(4,1)} %constant.101) | copy-start | bytes 292
  233.6 27.6 %all-to-all-start.6 = ((bf16[16,3,40,240]{3,2,1,0:T(8,128)(2,1)}), bf16[16,3,40,240]{3,2,1,0:T(8,128)(2,1)S(1)}, u32[]{:S(2)}, u32[]{:S(2)}) async-start(bf16[16,3,40,240]{3,2,1,0:T(8,128)(2,1)} %dft.23), calls=%async_computation.6 | async-start | bytes 1966080 | tf_op jit(solution)/shard_map/all_to_all | solution.py:255
  (22 other events, 60.9 us)
